TPU v7x, 32 devices: a whole 2x2x4 slice. The times are simulated.
32 devices in a mesh: row: 8 (over y, x, core), col: 4 (over z).
Axes of the slice: x: 2, y: 2, z: 4, core: 2. Of those that a mesh axis runs over, the one named last changes fastest.
Arguments:
- efield_x: float32 [32, 32, 512], P('row', 'col'), may hold values from -0.6 to 0.6
- efield_y: float32 [32, 32, 512], P('row', 'col'), may hold values from -0.6 to 0.6
- efield_z: float32 [32, 32, 512], P('row', 'col'), may hold values from -0.6 to 0.6
- hfield_x: float32 [32, 32, 512], P('row', 'col'), may hold values from -0.6 to 0.6
- hfield_y: float32 [32, 32, 512], P('row', 'col'), may hold values from -0.6 to 0.6
- hfield_z: float32 [32, 32, 512], P('row', 'col'), may hold values from -0.6 to 0.6
- permittivity: float32 [32, 32, 512], P('row', 'col'), may hold values from 1 to 4.4
- conductivity: float32 [32, 32, 512], P('row', 'col'), may hold values from 0.001 to 0.05
Outputs:
- next_ex: float32 [32, 32, 512], P('row', 'col')
- next_ey: float32 [32, 32, 512], P('row', 'col')
- next_ez: float32 [32, 32, 512], P('row', 'col')
- next_hx: float32 [32, 32, 512], P('row', 'col')
- next_hy: float32 [32, 32, 512], P('row', 'col')
- next_hz: float32 [32, 32, 512], P('row', 'col')
All inputs are finite; a program needn't handle non-finite values.
Results may differ from a plain program's by a relative error of at most 0.0055.
Values sent between devices are 32-bit elements; how exact they have to be, the bound alone decides.
A program may use at most 64 MiB of HBM per device.

v0:
```python
import jax
import jax.numpy as jnp
from jax import lax
from jax.sharding import PartitionSpec as P

HALF_STEP = 30.0


def with_halo(cells, sides, width):
    for axis, dim in sides:
        count = lax.axis_size(axis)
        ends = count - 1
        head = lax.slice_in_dim(cells, 0, width, axis=dim)
        tail = lax.slice_in_dim(cells, cells.shape[dim] - width, cells.shape[dim], axis=dim)
        cells = jnp.concatenate(
            [
                lax.ppermute(tail, axis, [(i, (i + 1) % count) for i in range(ends)]),
                cells,
                lax.ppermute(head, axis, [((i + 1) % count, i) for i in range(ends)]),
            ],
            axis=dim,
        )
    return cells


def shifted(values, stride, line_axis, filler, forward):
    length = values.shape[line_axis]
    padding = jnp.full_like(lax.slice_in_dim(values, 0, stride, axis=line_axis), filler)
    if forward:
        return jnp.concatenate(
            [lax.slice_in_dim(values, stride, length, axis=line_axis), padding], line_axis
        )
    return jnp.concatenate(
        [padding, lax.slice_in_dim(values, 0, length - stride, axis=line_axis)], line_axis
    )


def diff_up(values, line_axis):
    return shifted(values, 1, line_axis, 0.0, True) - values


def diff_down(values, line_axis):
    return values - shifted(values, 1, line_axis, 0.0, False)


def reduce_lines(sub_diag, main_diag, super_diag, source, line_axis):
    length = source.shape[line_axis]
    stride = 1
    while stride < length:
        sub_lo = shifted(sub_diag, stride, line_axis, 0.0, False)
        mid_lo = shifted(main_diag, stride, line_axis, 1.0, False)
        sup_lo = shifted(super_diag, stride, line_axis, 0.0, False)
        src_lo = shifted(source, stride, line_axis, 0.0, False)
        sub_hi = shifted(sub_diag, stride, line_axis, 0.0, True)
        mid_hi = shifted(main_diag, stride, line_axis, 1.0, True)
        sup_hi = shifted(super_diag, stride, line_axis, 0.0, True)
        src_hi = shifted(source, stride, line_axis, 0.0, True)
        ratio_lo = sub_diag / mid_lo
        ratio_hi = super_diag / mid_hi
        sub_diag = -sub_lo * ratio_lo
        super_diag = -sup_hi * ratio_hi
        main_diag = main_diag - sup_lo * ratio_lo - sub_hi * ratio_hi
        source = source - src_lo * ratio_lo - src_hi * ratio_hi
        stride = stride * 2
    return source / main_diag


def line_flags(length, line_axis, rank):
    iota_shape = [1] * rank
    iota_shape[line_axis] = length
    where_line = lax.broadcasted_iota(jnp.int32, tuple(iota_shape), line_axis)
    return (where_line == 0, where_line == length - 1)


def line_system(coupling, is_first, is_final):
    sub_diag = jnp.where(is_first, 0.0, -coupling)
    main_diag = jnp.where(is_first, 1.0 + coupling, 1.0 + 2.0 * coupling)
    super_diag = jnp.where(is_final, 0.0, -coupling)
    return (sub_diag, main_diag, super_diag)


def solve_local(source, coupling, line_axis):
    is_first, is_final = line_flags(source.shape[line_axis], line_axis, source.ndim)
    sub_diag, main_diag, super_diag = line_system(coupling, is_first, is_final)
    return reduce_lines(sub_diag, main_diag, super_diag, source, line_axis)


def inner(values):
    return values[1:-1, 1:-1]


def with_faces(stacked):
    return with_halo(stacked, (("row", 1), ("col", 2)), 1)


def inside_mask(count_y, count_z):
    pos_y = (
        lax.axis_index("row") * count_y
        + lax.broadcasted_iota(jnp.int32, (count_y + 2, 1, 1), 0)
        - 1
    )
    pos_z = (
        lax.axis_index("col") * count_z
        + lax.broadcasted_iota(jnp.int32, (1, count_z + 2, 1), 1)
        - 1
    )
    inside = (
        (pos_y >= 0)
        & (pos_y < count_y * lax.axis_size("row"))
        & (pos_z >= 0)
        & (pos_z < count_z * lax.axis_size("col"))
    )
    return inside.astype(jnp.float32)


def solve_rows_moved(source, coupling):

    def along_lines(pieces):
        moved_source, moved_coupling = pieces
        turned_source = jnp.transpose(moved_source, (1, 2, 0))
        turned_coupling = jnp.transpose(moved_coupling, (1, 2, 0))
        solved = solve_local(turned_source, turned_coupling, 2)
        solved = jnp.transpose(solved, (2, 0, 1))
        return lax.all_to_all(solved, "row", split_axis=0, concat_axis=2, tiled=True)

    return along_lines(
        (
            lax.all_to_all(source, "row", split_axis=2, concat_axis=0, tiled=True),
            lax.all_to_all(coupling, "row", split_axis=2, concat_axis=0, tiled=True),
        )
    )


def solve_rows(source, coupling):
    return solve_rows_moved(source, coupling)


def solve_columns(source, coupling):

    def along_lines(pieces):
        moved_source, moved_coupling = pieces
        solved = solve_local(moved_source, moved_coupling, 1)
        return lax.all_to_all(solved, "col", split_axis=1, concat_axis=2, tiled=True)

    return along_lines(
        (
            lax.all_to_all(source, "col", split_axis=2, concat_axis=1, tiled=True),
            lax.all_to_all(coupling, "col", split_axis=2, concat_axis=1, tiled=True),
        )
    )


def on_device(
    efield_x, efield_y, efield_z, hfield_x, hfield_y, hfield_z, permittivity, conductivity
):
    count_y = efield_x.shape[0]
    count_z = efield_x.shape[1]
    damping = conductivity * HALF_STEP / (2.0 * permittivity)
    keep_coef = (1.0 - damping) / (1.0 + damping)
    drive_coef = HALF_STEP / (permittivity * (1.0 + damping))
    coupling = drive_coef * HALF_STEP
    old_all = with_faces(jnp.stack([efield_x, efield_y, efield_z, hfield_x, hfield_y, hfield_z]))
    old_ex, old_ey, old_ez = (old_all[0], old_all[1], old_all[2])
    old_hx, old_hy, old_hz = (old_all[3], old_all[4], old_all[5])
    source_x = keep_coef * efield_x + drive_coef * (
        inner(diff_down(old_hz, 0))
        - inner(diff_down(old_hy, 1))
        - HALF_STEP * inner(diff_down(diff_up(old_ey, 2), 0))
    )
    source_y = keep_coef * efield_y + drive_coef * (
        inner(diff_down(old_hx, 1))
        - diff_down(hfield_z, 2)
        - HALF_STEP * inner(diff_down(diff_up(old_ez, 0), 1))
    )
    source_z = keep_coef * efield_z + drive_coef * (
        diff_down(hfield_y, 2)
        - inner(diff_down(old_hx, 0))
        - HALF_STEP * inner(diff_down(diff_up(old_ex, 1), 2))
    )
    half_ex = solve_rows(source_x, coupling)
    half_ey = solve_columns(source_y, coupling)
    half_ez = solve_local(source_z, coupling, 2)
    mid_all = with_faces(jnp.stack([half_ex, half_ey, half_ez]))
    mid_ex, mid_ey, mid_ez = (mid_all[0], mid_all[1], mid_all[2])
    inside = inside_mask(count_y, count_z)
    dz_mid_ey = diff_up(mid_ey, 1)
    dx_mid_ez = diff_up(mid_ez, 2)
    dy_mid_ex = diff_up(mid_ex, 0)
    mid_hx = (old_hx + HALF_STEP * (dz_mid_ey - diff_up(old_ez, 0))) * inside
    mid_hy = (old_hy + HALF_STEP * (dx_mid_ez - diff_up(old_ex, 1))) * inside
    mid_hz = (old_hz + HALF_STEP * (dy_mid_ex - diff_up(old_ey, 2))) * inside
    second_x = keep_coef * half_ex + drive_coef * (
        inner(diff_down(mid_hz, 0))
        - inner(diff_down(mid_hy, 1))
        - HALF_STEP * inner(diff_down(dx_mid_ez, 1))
    )
    second_y = keep_coef * half_ey + drive_coef * (
        inner(diff_down(mid_hx, 1))
        - inner(diff_down(mid_hz, 2))
        - HALF_STEP * inner(diff_down(dy_mid_ex, 2))
    )
    second_z = keep_coef * half_ez + drive_coef * (
        inner(diff_down(mid_hy, 2))
        - inner(diff_down(mid_hx, 0))
        - HALF_STEP * inner(diff_down(dz_mid_ey, 0))
    )
    next_ex = solve_columns(second_x, coupling)
    next_ey = solve_local(second_y, coupling, 2)
    next_ez = solve_rows(second_z, coupling)
    last_all = with_faces(jnp.stack([next_ex, next_ez]))
    next_hx = inner(mid_hx) + HALF_STEP * (inner(dz_mid_ey) - inner(diff_up(last_all[1], 0)))
    next_hy = inner(mid_hy) + HALF_STEP * (inner(dx_mid_ez) - inner(diff_up(last_all[0], 1)))
    next_hz = inner(mid_hz) + HALF_STEP * (inner(dy_mid_ex) - diff_up(next_ey, 2))
    return (next_ex, next_ey, next_ez, next_hx, next_hy, next_hz)


def solution(mesh):
    placed = (
        P("row", "col", None),
        P("row", "col", None),
        P("row", "col", None),
        P("row", "col", None),
        P("row", "col", None),
        P("row", "col", None),
        P("row", "col", None),
        P("row", "col", None),
    )
    return jax.shard_map(
        on_device,
        mesh=mesh,
        in_specs=placed,
        out_specs=(
            P("row", "col", None),
            P("row", "col", None),
            P("row", "col", None),
            P("row", "col", None),
            P("row", "col", None),
            P("row", "col", None),
        ),
        check_vma=False,
    )
```

profile of v0, /device:TPU:0, one launch (start us, length us, event | category | flops | bytes accessed | tf_op | source)
XLA Modules:
  0.0 173.5 jit_solution(10690655435091139427)
XLA Ops:
  0.6 0.8 bitcast_dynamic-update-slice_fusion.5
  1.5 0.8 bitcast_dynamic-update-slice_fusion.4
  2.3 0.8 bitcast_dynamic-update-slice_fusion.3
  3.2 0.8 bitcast_dynamic-update-slice_fusion.2
  4.0 0.8 bitcast_dynamic-update-slice_fusion.1
  4.9 0.8 bitcast_dynamic-update-slice_fusion
  5.7 2.4 %collective-permute-start = (f32[6,1,8,512]{3,2,1,0:T(8,128)S(1)}, f32[6,1,8,512]{3,2,1,0:T(8,128)S(1)}, u32[]{:S(2)}, u32[]{:S(2)}) collective-permute-start(f32[6,1,8,512]{3,2,1,0:T(8,128)S(1)} %get-tuple-element.113), channel_id=1, source_target_pairs={{0,4},{4,8},{8,12},{12,16},{16,20},{20,24},{24,28},{1,5},{5,9},{9,... | collective-permute-start | bytes 294920 | tf_op jit(solution)/shard_map/ppermute | solution.py:17
  8.1 1.3 collective-permute-start.1
  9.4 3.9 %collective-permute-done.1 = f32[6,1,8,512]{3,2,1,0:T(8,128)S(1)} collective-permute-done((f32[6,1,8,512]{3,2,1,0:T(8,128)S(1)}, f32[6,1,8,512]{3,2,1,0:T(8,128)S(1)}, u32[]{:S(2)}, u32[]{:S(2)}) %collective-permute-start.1) | collective-permute-done | bytes 98336 | tf_op jit(solution)/shard_map/ppermute | solution.py:19
  13.5 3.5 %collective-permute-start.2 = (f32[6,6,1,512]{3,2,1,0:T(1,128)S(1)}, f32[6,6,1,512]{3,2,1,0:T(1,128)S(1)}, u32[]{:S(2)}, u32[]{:S(2)}) collective-permute-start(f32[6,6,1,512]{3,2,1,0:T(1,128)S(1)} %get-tuple-element.109), channel_id=1, source_target_pairs={{0,1},{1,2},{2,3},{4,5},{5,6},{6,7},{8,9},{9,10},{10,11},{12,13},{... | collective-permute-start | bytes 221192 | tf_op jit(solution)/shard_map/ppermute | solution.py:17
  17.0 1.3 collective-permute-start.3
  18.9 4.3 %collective-permute-done.3 = f32[6,6,1,512]{3,2,1,0:T(1,128)S(1)} collective-permute-done((f32[6,6,1,512]{3,2,1,0:T(1,128)S(1)}, f32[6,6,1,512]{3,2,1,0:T(1,128)S(1)}, u32[]{:S(2)}, u32[]{:S(2)}) %collective-permute-start.3) | collective-permute-done | bytes 73760 | tf_op jit(solution)/shard_map/ppermute | solution.py:19
  30.8 1.8 %reshape.160 = f32[8,1,2048]{2,1,0:T(1,128)} reshape(f32[512,4,8]{2,1,0:T(4,128)S(1)} %bitcast.199) | data formatting | bytes 131072
  32.6 5.6 %all-to-all-start = ((f32[8,1,2048]{2,1,0:T(1,128)}), f32[8,1,2048]{2,1,0:T(1,128)S(1)}, u32[]{:S(2)}, u32[]{:S(2)}) async-start(f32[8,1,2048]{2,1,0:T(1,128)} %reshape.160), calls=%async_computation | async-start | bytes 131072 | tf_op jit(solution)/shard_map/all_to_all | solution.py:128
  40.5 1.8 %reshape.156 = f32[4,1,4096]{2,1,0:T(1,128)} reshape(f32[512,4,8]{2,1,0:T(4,128)S(1)} %bitcast.200) | data formatting | bytes 131072
  42.6 1.8 %reshape.158 = f32[8,1,2048]{2,1,0:T(1,128)} reshape(f32[512,4,8]{2,1,0:T(4,128)S(1)} %bitcast.195) | data formatting | bytes 131072
  44.4 1.8 %reshape.154 = f32[4,1,4096]{2,1,0:T(1,128)} reshape(f32[512,4,8]{2,1,0:T(4,128)S(1)} %bitcast.196) | data formatting | bytes 131072
  46.2 4.2 %all-to-all-start.1 = ((f32[8,1,2048]{2,1,0:T(1,128)}), f32[8,1,2048]{2,1,0:T(1,128)S(1)}, u32[]{:S(2)}, u32[]{:S(2)}) async-start(f32[8,1,2048]{2,1,0:T(1,128)} %reshape.158), calls=%async_computation.1 | async-start | bytes 131072 | tf_op jit(solution)/shard_map/all_to_all | solution.py:129
  50.9 0.8 reduce.2
  51.7 1.2 reshape.161
  53.3 2.1 %all-to-all-done.1 = f32[8,1,2048]{2,1,0:T(1,128)S(1)} async-done(((f32[8,1,2048]{2,1,0:T(1,128)}), f32[8,1,2048]{2,1,0:T(1,128)S(1)}, u32[]{:S(2)}, u32[]{:S(2)}) %all-to-all-start.1) | async-done | bytes 65568 | tf_op jit(solution)/shard_map/all_to_all | solution.py:129
  55.4 3.9 %all-to-all-start.3 = ((f32[4,1,4096]{2,1,0:T(1,128)}), f32[4,1,4096]{2,1,0:T(1,128)S(1)}, u32[]{:S(2)}, u32[]{:S(2)}) async-start(f32[4,1,4096]{2,1,0:T(1,128)} %reshape.156), calls=%async_computation.3 | async-start | bytes 131072 | tf_op jit(solution)/shard_map/all_to_all | solution.py:147
  59.2 0.8 reduce.3
  60.0 1.2 reshape.159
  65.4 0.8 reshape.162
  66.2 5.1 %all-to-all-start.4 = ((f32[4,1,4096]{2,1,0:T(1,128)}), f32[4,1,4096]{2,1,0:T(1,128)S(1)}, u32[]{:S(2)}, u32[]{:S(2)}) async-start(f32[4,1,4096]{2,1,0:T(1,128)} %reshape.154), calls=%async_computation.4 | async-start | bytes 131072 | tf_op jit(solution)/shard_map/all_to_all | solution.py:148
  71.3 0.8 reduce
  72.1 1.3 reshape.157
  74.4 2.7 %all-to-all-done.4 = f32[4,1,4096]{2,1,0:T(1,128)S(1)} async-done(((f32[4,1,4096]{2,1,0:T(1,128)}), f32[4,1,4096]{2,1,0:T(1,128)S(1)}, u32[]{:S(2)}, u32[]{:S(2)}) %all-to-all-start.4) | async-done | bytes 65568 | tf_op jit(solution)/shard_map/all_to_all | solution.py:148
  77.0 4.0 %all-to-all-start.2 = ((f32[8,1,2048]{2,1,0:T(1,128)}), f32[8,1,2048]{2,1,0:T(1,128)}, u32[]{:S(2)}, u32[]{:S(2)}) async-start(f32[8,1,2048]{2,1,0:T(1,128)} %reshape.162), calls=%async_computation.2 | async-start | bytes 131072 | tf_op jit(solution)/shard_map/all_to_all | solution.py:124
  81.0 0.8 reduce.1
  81.8 1.3 reshape.155
  83.3 1.0 copy.68
  84.3 0.9 add_bitcast_fusion.1
  88.7 3.3 %all-to-all-start.5 = ((f32[4,32,128]{2,0,1:T(4,128)}), f32[4,32,128]{2,0,1:T(4,128)S(1)}, u32[]{:S(2)}, u32[]{:S(2)}) async-start(f32[4,32,128]{2,0,1:T(4,128)} %subtract_divide_fusion.3), calls=%async_computation.5 | async-start | bytes 131072 | tf_op jit(solution)/shard_map/all_to_all | solution.py:143
  92.1 1.6 reduce.4
  94.1 3.6 %all-to-all-done.5 = f32[4,32,128]{2,0,1:T(4,128)S(1)} async-done(((f32[4,32,128]{2,0,1:T(4,128)}), f32[4,32,128]{2,0,1:T(4,128)S(1)}, u32[]{:S(2)}, u32[]{:S(2)}) %all-to-all-start.5) | async-done | bytes 65568 | tf_op jit(solution)/shard_map/all_to_all | solution.py:143
  97.7 1.3 collective-permute-start.4
  99.0 1.3 collective-permute-start.5
  100.4 3.9 %collective-permute-done.5 = f32[3,1,8,512]{3,2,1,0:T(8,128)S(1)} collective-permute-done((f32[3,1,8,512]{3,2,1,0:T(8,128)S(1)}, f32[3,1,8,512]{3,2,1,0:T(8,128)S(1)}, u32[]{:S(2)}, u32[]{:S(2)}) %collective-permute-start.5) | collective-permute-done | bytes 49184 | tf_op jit(solution)/shard_map/ppermute | solution.py:19
  104.3 2.8 %collective-permute-start.6 = (f32[3,6,1,512]{3,2,1,0:T(1,128)S(1)}, f32[3,6,1,512]{3,2,1,0:T(1,128)S(1)}, u32[]{:S(2)}, u32[]{:S(2)}) collective-permute-start(f32[3,6,1,512]{3,2,1,0:T(1,128)S(1)} %get-tuple-element.119), channel_id=1, source_target_pairs={{0,1},{1,2},{2,3},{4,5},{5,6},{6,7},{8,9},{9,10},{10,11},{12,13},{... | collective-permute-start | bytes 110600 | tf_op jit(solution)/shard_map/ppermute | solution.py:17
  107.1 1.3 collective-permute-start.7
  109.2 3.8 %collective-permute-done.7 = f32[3,6,1,512]{3,2,1,0:T(1,128)S(1)} collective-permute-done((f32[3,6,1,512]{3,2,1,0:T(1,128)S(1)}, f32[3,6,1,512]{3,2,1,0:T(1,128)S(1)}, u32[]{:S(2)}, u32[]{:S(2)}) %collective-permute-start.7) | collective-permute-done | bytes 36896 | tf_op jit(solution)/shard_map/ppermute | solution.py:19
  118.2 1.8 %reshape.166 = f32[8,1,2048]{2,1,0:T(1,128)} reshape(f32[512,4,8]{2,1,0:T(4,128)S(1)} %bitcast.204) | data formatting | bytes 131072
  120.0 4.9 %all-to-all-start.8 = ((f32[8,1,2048]{2,1,0:T(1,128)}), f32[8,1,2048]{2,1,0:T(1,128)S(1)}, u32[]{:S(2)}, u32[]{:S(2)}) async-start(f32[8,1,2048]{2,1,0:T(1,128)} %reshape.166), calls=%async_computation.8 | async-start | bytes 131072 | tf_op jit(solution)/shard_map/all_to_all | solution.py:128
  126.0 1.8 %reshape.164 = f32[4,1,4096]{2,1,0:T(1,128)} reshape(f32[512,4,8]{2,1,0:T(4,128)S(1)} %bitcast.205) | data formatting | bytes 131072
  127.8 2.1 %all-to-all-done.8 = f32[8,1,2048]{2,1,0:T(1,128)S(1)} async-done(((f32[8,1,2048]{2,1,0:T(1,128)}), f32[8,1,2048]{2,1,0:T(1,128)S(1)}, u32[]{:S(2)}, u32[]{:S(2)}) %all-to-all-start.8) | async-done | bytes 65568 | tf_op jit(solution)/shard_map/all_to_all | solution.py:128
  129.9 3.3 %all-to-all-start.6 = ((f32[4,1,4096]{2,1,0:T(1,128)}), f32[4,1,4096]{2,1,0:T(1,128)S(1)}, u32[]{:S(2)}, u32[]{:S(2)}) async-start(f32[4,1,4096]{2,1,0:T(1,128)} %reshape.164), calls=%async_computation.6 | async-start | bytes 131072 | tf_op jit(solution)/shard_map/all_to_all | solution.py:147
  133.2 0.8 reduce.6
  134.0 1.2 reshape.167
  135.7 0.8 copy-done.9
  138.9 3.3 %all-to-all-start.9 = ((f32[8,1,2048]{2,1,0:T(1,128)}), f32[8,1,2048]{2,1,0:T(1,128)S(1)}, u32[]{:S(2)}, u32[]{:S(2)}) async-start(f32[8,1,2048]{2,1,0:T(1,128)} %reshape.168), calls=%async_computation.9 | async-start | bytes 131072 | tf_op jit(solution)/shard_map/all_to_all | solution.py:124
  142.2 0.8 reduce.5
  143.1 1.3 reshape.165
  146.4 0.8 all-to-all-done.9
  147.2 4.7 %all-to-all-start.7 = ((f32[4,32,128]{2,0,1:T(4,128)}), f32[4,32,128]{2,0,1:T(4,128)S(1)}, u32[]{:S(2)}, u32[]{:S(2)}) async-start(f32[4,32,128]{2,0,1:T(4,128)} %subtract_divide_fusion.1), calls=%async_computation.7 | async-start | bytes 131072 | tf_op jit(solution)/shard_map/all_to_all | solution.py:143
  151.9 0.8 reduce.7
  153.0 4.7 %all-to-all-done.7 = f32[4,32,128]{2,0,1:T(4,128)S(1)} async-done(((f32[4,32,128]{2,0,1:T(4,128)}), f32[4,32,128]{2,0,1:T(4,128)S(1)}, u32[]{:S(2)}, u32[]{:S(2)}) %all-to-all-start.7) | async-done | bytes 65568 | tf_op jit(solution)/shard_map/all_to_all | solution.py:143
  157.7 1.3 collective-permute-start.8
  159.0 1.3 collective-permute-start.9
  160.3 3.2 %collective-permute-done.9 = f32[2,1,8,512]{3,2,1,0:T(8,128)S(1)} collective-permute-done((f32[2,1,8,512]{3,2,1,0:T(8,128)S(1)}, f32[2,1,8,512]{3,2,1,0:T(8,128)S(1)}, u32[]{:S(2)}, u32[]{:S(2)}) %collective-permute-start.9) | collective-permute-done | bytes 32800 | tf_op jit(solution)/shard_map/ppermute | solution.py:19
  163.5 2.8 %collective-permute-start.10 = (f32[2,6,1,512]{3,2,1,0:T(1,128)S(1)}, f32[2,6,1,512]{3,2,1,0:T(1,128)S(1)}, u32[]{:S(2)}, u32[]{:S(2)}) collective-permute-start(f32[2,6,1,512]{3,2,1,0:T(1,128)S(1)} %get-tuple-element.123), channel_id=1, source_target_pairs={{0,1},{1,2},{2,3},{4,5},{5,6},{6,7},{8,9},{9,10},{10,11},{12,13},{... | collective-permute-start | bytes 73736 | tf_op jit(solution)/shard_map/ppermute | solution.py:17
  166.3 1.3 collective-permute-start.11
  168.3 3.7 %collective-permute-done.11 = f32[2,6,1,512]{3,2,1,0:T(1,128)S(1)} collective-permute-done((f32[2,6,1,512]{3,2,1,0:T(1,128)S(1)}, f32[2,6,1,512]{3,2,1,0:T(1,128)S(1)}, u32[]{:S(2)}, u32[]{:S(2)}) %collective-permute-start.11) | collective-permute-done | bytes 24608 | tf_op jit(solution)/shard_map/ppermute | solution.py:19
  (501 shorter events, 33.9 us)
Async XLA Ops:
  5.7 3.7 %collective-permute-start = (f32[6,1,8,512]{3,2,1,0:T(8,128)S(1)}, f32[6,1,8,512]{3,2,1,0:T(8,128)S(1)}, u32[]{:S(2)}, u32[]{:S(2)}) collective-permute-start(f32[6,1,8,512]{3,2,1,0:T(8,128)S(1)} %get-tuple-element.113), channel_id=1, source_target_pairs={{0,4},{4,8},{8,12},{12,16},{16,20},{20,24},{24,28},{1,5},{5,9},{9,... | collective-permute-start | bytes 294920 | tf_op jit(solution)/shard_map/ppermute | solution.py:17
  8.1 5.3 %collective-permute-start.1 = (f32[6,1,8,512]{3,2,1,0:T(8,128)S(1)}, f32[6,1,8,512]{3,2,1,0:T(8,128)S(1)}, u32[]{:S(2)}, u32[]{:S(2)}) collective-permute-start(f32[6,1,8,512]{3,2,1,0:T(8,128)S(1)} %get-tuple-element.114), channel_id=1, source_target_pairs={{4,0},{8,4},{12,8},{16,12},{20,16},{24,20},{28,24},{5,1},{9,5},{13... | collective-permute-start | bytes 294920 | tf_op jit(solution)/shard_map/ppermute | solution.py:19
  13.5 5.5 %collective-permute-start.2 = (f32[6,6,1,512]{3,2,1,0:T(1,128)S(1)}, f32[6,6,1,512]{3,2,1,0:T(1,128)S(1)}, u32[]{:S(2)}, u32[]{:S(2)}) collective-permute-start(f32[6,6,1,512]{3,2,1,0:T(1,128)S(1)} %get-tuple-element.109), channel_id=1, source_target_pairs={{0,1},{1,2},{2,3},{4,5},{5,6},{6,7},{8,9},{9,10},{10,11},{12,13},{... | collective-permute-start | bytes 221192 | tf_op jit(solution)/shard_map/ppermute | solution.py:17
  17.0 6.2 %collective-permute-start.3 = (f32[6,6,1,512]{3,2,1,0:T(1,128)S(1)}, f32[6,6,1,512]{3,2,1,0:T(1,128)S(1)}, u32[]{:S(2)}, u32[]{:S(2)}) collective-permute-start(f32[6,6,1,512]{3,2,1,0:T(1,128)S(1)} %get-tuple-element.110), channel_id=1, source_target_pairs={{1,0},{2,1},{3,2},{5,4},{6,5},{7,6},{9,8},{10,9},{11,10},{13,12},{... | collective-permute-start | bytes 221192 | tf_op jit(solution)/shard_map/ppermute | solution.py:19
  29.3 1.1 copy-start.96
  29.7 8.5 %copy-start.57 = (f32[4,8,512]{2,1,0:T(8,128)}, f32[4,8,512]{2,1,0:T(8,128)S(1)}, u32[]{:S(2)}) copy-start(f32[4,8,512]{2,1,0:T(8,128)S(1)} %get-tuple-element.54) | copy-start | bytes 196612
  29.7 9.2 %copy-start.68 = (f32[4,8,512]{2,1,0:T(8,128)}, f32[4,8,512]{2,1,0:T(8,128)S(1)}, u32[]{:S(2)}) copy-start(f32[4,8,512]{2,1,0:T(8,128)S(1)} %get-tuple-element.53) | copy-start | bytes 196612
  29.7 2.9 %copy-start.61 = (f32[4,8,512]{2,1,0:T(8,128)}, f32[4,8,512]{2,1,0:T(8,128)S(1)}, u32[]{:S(2)}) copy-start(f32[4,8,512]{2,1,0:T(8,128)S(1)} %get-tuple-element.55) | copy-start | bytes 196612
  29.7 8.4 %copy-start.102 = (f32[4,8,512]{2,1,0:T(8,128)}, f32[4,8,512]{2,1,0:T(8,128)S(1)}, u32[]{:S(2)}) copy-start(f32[4,8,512]{2,1,0:T(8,128)S(1)} %get-tuple-element.56) | copy-start | bytes 196612
  32.6 13.6 %all-to-all-start = ((f32[8,1,2048]{2,1,0:T(1,128)}), f32[8,1,2048]{2,1,0:T(1,128)S(1)}, u32[]{:S(2)}, u32[]{:S(2)}) async-start(f32[8,1,2048]{2,1,0:T(1,128)} %reshape.160), calls=%async_computation | async-start | bytes 131072 | tf_op jit(solution)/shard_map/all_to_all | solution.py:128
  38.2 4.0 %copy-start.73 = (f32[4,8,512]{2,1,0:T(8,128)}, f32[4,8,512]{2,1,0:T(8,128)S(1)}, u32[]{:S(2)}) copy-start(f32[4,8,512]{2,1,0:T(8,128)S(1)} %get-tuple-element.230) | copy-start | bytes 196612
  38.2 4.0 %copy-start.100 = (f32[4,8,512]{2,1,0:T(8,128)}, f32[4,8,512]{2,1,0:T(8,128)S(1)}, u32[]{:S(2)}) copy-start(f32[4,8,512]{2,1,0:T(8,128)S(1)} %get-tuple-element.231) | copy-start | bytes 196612
  46.2 9.2 %all-to-all-start.1 = ((f32[8,1,2048]{2,1,0:T(1,128)}), f32[8,1,2048]{2,1,0:T(1,128)S(1)}, u32[]{:S(2)}, u32[]{:S(2)}) async-start(f32[8,1,2048]{2,1,0:T(1,128)} %reshape.158), calls=%async_computation.1 | async-start | bytes 131072 | tf_op jit(solution)/shard_map/all_to_all | solution.py:129
  55.4 10.8 %all-to-all-start.3 = ((f32[4,1,4096]{2,1,0:T(1,128)}), f32[4,1,4096]{2,1,0:T(1,128)S(1)}, u32[]{:S(2)}, u32[]{:S(2)}) async-start(f32[4,1,4096]{2,1,0:T(1,128)} %reshape.156), calls=%async_computation.3 | async-start | bytes 131072 | tf_op jit(solution)/shard_map/all_to_all | solution.py:147
  65.3 6.1 %copy-start.18 = (f32[8,64,32]{1,0,2:T(8,128)}, f32[8,64,32]{1,0,2:T(8,128)S(1)}, u32[]{:S(2)}) copy-start(f32[8,64,32]{1,0,2:T(8,128)S(1)} %get-tuple-element.141) | copy-start | bytes 196612
  65.3 6.0 %copy-start.83 = (f32[8,64,16]{1,0,2:T(8,128)}, f32[8,64,16]{1,0,2:T(8,128)S(1)}, u32[]{:S(2)}) copy-start(f32[8,64,16]{1,0,2:T(8,128)S(1)} %slice.1217) | copy-start | bytes 98308
  65.3 6.0 %copy-start.87 = (f32[8,64,16]{1,0,2:T(8,128)}, f32[8,64,16]{1,0,2:T(8,128)S(1)}, u32[]{:S(2)}) copy-start(f32[8,64,16]{1,0,2:T(8,128)S(1)} %get-tuple-element.139) | copy-start | bytes 98308
  65.3 6.0 %copy-start.89 = (f32[8,64,16]{1,0,2:T(8,128)}, f32[8,64,16]{1,0,2:T(8,128)S(1)}, u32[]{:S(2)}) copy-start(f32[8,64,16]{1,0,2:T(8,128)S(1)} %get-tuple-element.140) | copy-start | bytes 98308
  66.2 10.8 %all-to-all-start.4 = ((f32[4,1,4096]{2,1,0:T(1,128)}), f32[4,1,4096]{2,1,0:T(1,128)S(1)}, u32[]{:S(2)}, u32[]{:S(2)}) async-start(f32[4,1,4096]{2,1,0:T(1,128)} %reshape.154), calls=%async_computation.4 | async-start | bytes 131072 | tf_op jit(solution)/shard_map/all_to_all | solution.py:148
  73.7 8.1 %copy-start.66 = (f32[4,4,8,128]{3,0,2,1:T(4,128)}, f32[4,4,8,128]{3,0,2,1:T(4,128)S(1)}, u32[]{:S(2)}) copy-start(f32[4,4,8,128]{3,0,2,1:T(4,128)S(1)} %copy.65) | copy-start | bytes 196612
  77.0 11.6 %all-to-all-start.2 = ((f32[8,1,2048]{2,1,0:T(1,128)}), f32[8,1,2048]{2,1,0:T(1,128)}, u32[]{:S(2)}, u32[]{:S(2)}) async-start(f32[8,1,2048]{2,1,0:T(1,128)} %reshape.162), calls=%async_computation.2 | async-start | bytes 131072 | tf_op jit(solution)/shard_map/all_to_all | solution.py:124
  84.3 1.4 copy-start.67
  84.3 1.4 copy-start.126
  84.3 1.5 copy-start.127
  87.5 1.1 copy-start.59
  87.5 1.1 copy-start.71
  87.6 4.4 %copy-start.62 = (f32[4,8,512]{2,1,0:T(8,128)S(1)}, f32[4,8,512]{2,1,0:T(8,128)}, u32[]{:S(2)}) copy-start(f32[4,8,512]{2,1,0:T(8,128)} %copy-done.61) | copy-start | bytes 196612
  87.6 4.4 %copy-start.69 = (f32[4,8,512]{2,1,0:T(8,128)S(1)}, f32[4,8,512]{2,1,0:T(8,128)}, u32[]{:S(2)}) copy-start(f32[4,8,512]{2,1,0:T(8,128)} %copy-done.68) | copy-start | bytes 196612
  87.6 4.4 %copy-start.74 = (f32[4,8,512]{2,1,0:T(8,128)S(1)}, f32[4,8,512]{2,1,0:T(8,128)}, u32[]{:S(2)}) copy-start(f32[4,8,512]{2,1,0:T(8,128)} %copy-done.73) | copy-start | bytes 196612
  87.6 4.4 %copy-start.101 = (f32[4,8,512]{2,1,0:T(8,128)S(1)}, f32[4,8,512]{2,1,0:T(8,128)}, u32[]{:S(2)}) copy-start(f32[4,8,512]{2,1,0:T(8,128)} %copy-done.100) | copy-start | bytes 196612
  87.6 4.4 %copy-start.106 = (f32[4,8,256]{2,1,0:T(8,128)S(1)}, f32[4,8,256]{2,1,0:T(8,128)}, u32[]{:S(2)}) copy-start(f32[4,8,256]{2,1,0:T(8,128)} %slice.1337) | copy-start | bytes 98308
  87.6 4.4 %copy-start.108 = (f32[4,8,256]{2,1,0:T(8,128)S(1)}, f32[4,8,256]{2,1,0:T(8,128)}, u32[]{:S(2)}) copy-start(f32[4,8,256]{2,1,0:T(8,128)} %slice.1338) | copy-start | bytes 98308
  87.6 4.4 %copy-start.114 = (f32[4,8,256]{2,1,0:T(8,128)S(1)}, f32[4,8,256]{2,1,0:T(8,128)}, u32[]{:S(2)}) copy-start(f32[4,8,256]{2,1,0:T(8,128)} %get-tuple-element.228) | copy-start | bytes 98308
  87.6 4.4 %copy-start.116 = (f32[4,8,256]{2,1,0:T(8,128)S(1)}, f32[4,8,256]{2,1,0:T(8,128)}, u32[]{:S(2)}) copy-start(f32[4,8,256]{2,1,0:T(8,128)} %get-tuple-element.229) | copy-start | bytes 98308
  87.7 4.4 %copy-start.128 = (f32[4,8,256]{2,1,0:T(8,128)S(1)}, f32[4,8,256]{2,1,0:T(8,128)}, u32[]{:S(2)}) copy-start(f32[4,8,256]{2,1,0:T(8,128)} %get-tuple-element.234) | copy-start | bytes 98308
  87.7 4.4 %copy-start.129 = (f32[4,8,256]{2,1,0:T(8,128)S(1)}, f32[4,8,256]{2,1,0:T(8,128)}, u32[]{:S(2)}) copy-start(f32[4,8,256]{2,1,0:T(8,128)} %get-tuple-element.235) | copy-start | bytes 98308
  87.8 6.1 %copy-start.64 = (f32[4,32,128]{2,0,1:T(4,128)}, f32[4,32,128]{2,0,1:T(4,128)S(1)}, u32[]{:S(2)}) copy-start(f32[4,32,128]{2,0,1:T(4,128)S(1)} %get-tuple-element.36) | copy-start | bytes 196612
  87.8 6.2 %copy-start.104 = (f32[4,32,128]{2,0,1:T(4,128)}, f32[4,32,128]{2,0,1:T(4,128)S(1)}, u32[]{:S(2)}) copy-start(f32[4,32,128]{2,0,1:T(4,128)S(1)} %get-tuple-element.37) | copy-start | bytes 196612
  87.9 6.0 %copy-start.76 = (f32[4,32,128]{2,0,1:T(4,128)}, f32[4,32,128]{2,0,1:T(4,128)S(1)}, u32[]{:S(2)}) copy-start(f32[4,32,128]{2,0,1:T(4,128)S(1)} %get-tuple-element.216) | copy-start | bytes 196612
  87.9 4.2 %copy-start.112 = (f32[4,16,128]{2,0,1:T(4,128)}, f32[4,16,128]{2,0,1:T(4,128)S(1)}, u32[]{:S(2)}) copy-start(f32[4,16,128]{2,0,1:T(4,128)S(1)} %slice.1262) | copy-start | bytes 98308
  87.9 4.2 %copy-start.118 = (f32[4,16,128]{2,0,1:T(4,128)}, f32[4,16,128]{2,0,1:T(4,128)S(1)}, u32[]{:S(2)}) copy-start(f32[4,16,128]{2,0,1:T(4,128)S(1)} %get-tuple-element.214) | copy-start | bytes 98308
  87.9 9.8 %copy-start.120 = (f32[4,16,128]{2,0,1:T(4,128)}, f32[4,16,128]{2,0,1:T(4,128)S(1)}, u32[]{:S(2)}) copy-start(f32[4,16,128]{2,0,1:T(4,128)S(1)} %get-tuple-element.215) | copy-start | bytes 98308
  88.7 9.0 %all-to-all-start.5 = ((f32[4,32,128]{2,0,1:T(4,128)}), f32[4,32,128]{2,0,1:T(4,128)S(1)}, u32[]{:S(2)}, u32[]{:S(2)}) async-start(f32[4,32,128]{2,0,1:T(4,128)} %subtract_divide_fusion.3), calls=%async_computation.5 | async-start | bytes 131072 | tf_op jit(solution)/shard_map/all_to_all | solution.py:143
  97.7 15.4 %copy-start.93 = (f32[4,32,128]{2,0,1:T(4,128)}, f32[4,32,128]{2,0,1:T(4,128)S(1)}, u32[]{:S(2)}) copy-start(f32[4,32,128]{2,0,1:T(4,128)S(1)} %all-to-all-done.5) | copy-start | bytes 196612
  97.7 2.6 %collective-permute-start.4 = (f32[3,1,8,512]{3,2,1,0:T(8,128)S(1)}, f32[3,1,8,512]{3,2,1,0:T(8,128)S(1)}, u32[]{:S(2)}, u32[]{:S(2)}) collective-permute-start(f32[3,1,8,512]{3,2,1,0:T(8,128)S(1)} %get-tuple-element.125), channel_id=1, source_target_pairs={{0,4},{4,8},{8,12},{12,16},{16,20},{20,24},{24,28},{1,5},{5,9},{9,... | collective-permute-start | bytes 147464 | tf_op jit(solution)/shard_map/ppermute | solution.py:17
  99.0 5.2 %collective-permute-start.5 = (f32[3,1,8,512]{3,2,1,0:T(8,128)S(1)}, f32[3,1,8,512]{3,2,1,0:T(8,128)S(1)}, u32[]{:S(2)}, u32[]{:S(2)}) collective-permute-start(f32[3,1,8,512]{3,2,1,0:T(8,128)S(1)} %get-tuple-element.126), channel_id=1, source_target_pairs={{4,0},{8,4},{12,8},{16,12},{20,16},{24,20},{28,24},{5,1},{9,5},{13... | collective-permute-start | bytes 147464 | tf_op jit(solution)/shard_map/ppermute | solution.py:19
  104.3 4.9 %collective-permute-start.6 = (f32[3,6,1,512]{3,2,1,0:T(1,128)S(1)}, f32[3,6,1,512]{3,2,1,0:T(1,128)S(1)}, u32[]{:S(2)}, u32[]{:S(2)}) collective-permute-start(f32[3,6,1,512]{3,2,1,0:T(1,128)S(1)} %get-tuple-element.119), channel_id=1, source_target_pairs={{0,1},{1,2},{2,3},{4,5},{5,6},{6,7},{8,9},{9,10},{10,11},{12,13},{... | collective-permute-start | bytes 110600 | tf_op jit(solution)/shard_map/ppermute | solution.py:17
  107.1 5.9 %collective-permute-start.7 = (f32[3,6,1,512]{3,2,1,0:T(1,128)S(1)}, f32[3,6,1,512]{3,2,1,0:T(1,128)S(1)}, u32[]{:S(2)}, u32[]{:S(2)}) collective-permute-start(f32[3,6,1,512]{3,2,1,0:T(1,128)S(1)} %get-tuple-element.120), channel_id=1, source_target_pairs={{1,0},{2,1},{3,2},{5,4},{6,5},{7,6},{9,8},{10,9},{11,10},{13,12},{... | collective-permute-start | bytes 110600 | tf_op jit(solution)/shard_map/ppermute | solution.py:19
  117.7 7.1 %copy-start.95 = (f32[4,8,512]{2,1,0:T(8,128)}, f32[4,8,512]{2,1,0:T(8,128)S(1)}, u32[]{:S(2)}) copy-start(f32[4,8,512]{2,1,0:T(8,128)S(1)} %subtract_divide_fusion) | copy-start | bytes 196612
  117.8 7.0 %copy-start.78 = (f32[5,10,512]{2,1,0:T(8,128)S(1)}, f32[5,10,512]{2,1,0:T(8,128)}, u32[]{:S(2)}) copy-start(f32[5,10,512]{2,1,0:T(8,128)} %slice.1341) | copy-start | bytes 307204
  117.8 7.0 %copy-start.122 = (f32[4,8,512]{2,1,0:T(8,128)S(1)}, f32[4,8,512]{2,1,0:T(8,128)}, u32[]{:S(2)}) copy-start(f32[4,8,512]{2,1,0:T(8,128)} %all_to_all.136) | copy-start | bytes 196612
  120.0 9.9 %all-to-all-start.8 = ((f32[8,1,2048]{2,1,0:T(1,128)}), f32[8,1,2048]{2,1,0:T(1,128)S(1)}, u32[]{:S(2)}, u32[]{:S(2)}) async-start(f32[8,1,2048]{2,1,0:T(1,128)} %reshape.166), calls=%async_computation.8 | async-start | bytes 131072 | tf_op jit(solution)/shard_map/all_to_all | solution.py:128
  129.9 9.0 %all-to-all-start.6 = ((f32[4,1,4096]{2,1,0:T(1,128)}), f32[4,1,4096]{2,1,0:T(1,128)S(1)}, u32[]{:S(2)}, u32[]{:S(2)}) async-start(f32[4,1,4096]{2,1,0:T(1,128)} %reshape.164), calls=%async_computation.6 | async-start | bytes 131072 | tf_op jit(solution)/shard_map/all_to_all | solution.py:147
  134.0 1.6 copy-start.5
  134.0 1.6 copy-start.7
  138.9 8.3 %all-to-all-start.9 = ((f32[8,1,2048]{2,1,0:T(1,128)}), f32[8,1,2048]{2,1,0:T(1,128)S(1)}, u32[]{:S(2)}, u32[]{:S(2)}) async-start(f32[8,1,2048]{2,1,0:T(1,128)} %reshape.168), calls=%async_computation.9 | async-start | bytes 131072 | tf_op jit(solution)/shard_map/all_to_all | solution.py:124
  143.0 1.7 copy-start.54
  143.0 1.7 copy-start.56
  147.2 10.5 %all-to-all-start.7 = ((f32[4,32,128]{2,0,1:T(4,128)}), f32[4,32,128]{2,0,1:T(4,128)S(1)}, u32[]{:S(2)}, u32[]{:S(2)}) async-start(f32[4,32,128]{2,0,1:T(4,128)} %subtract_divide_fusion.1), calls=%async_computation.7 | async-start | bytes 131072 | tf_op jit(solution)/shard_map/all_to_all | solution.py:143
  157.7 14.5 %copy-start.50 = (f32[4,4,8,128]{3,2,1,0:T(8,128)}, f32[4,4,8,128]{3,2,1,0:T(8,128)S(1)}, u32[]{:S(2)}) copy-start(f32[4,4,8,128]{3,2,1,0:T(8,128)S(1)} %copy.89) | copy-start | bytes 196612
  157.7 2.6 %collective-permute-start.8 = (f32[2,1,8,512]{3,2,1,0:T(8,128)S(1)}, f32[2,1,8,512]{3,2,1,0:T(8,128)S(1)}, u32[]{:S(2)}, u32[]{:S(2)}) collective-permute-start(f32[2,1,8,512]{3,2,1,0:T(8,128)S(1)} %get-tuple-element.127), channel_id=1, source_target_pairs={{0,4},{4,8},{8,12},{12,16},{16,20},{20,24},{24,28},{1,5},{5,9},{9,... | collective-permute-start | bytes 98312 | tf_op jit(solution)/shard_map/ppermute | solution.py:17
  159.0 4.5 %collective-permute-start.9 = (f32[2,1,8,512]{3,2,1,0:T(8,128)S(1)}, f32[2,1,8,512]{3,2,1,0:T(8,128)S(1)}, u32[]{:S(2)}, u32[]{:S(2)}) collective-permute-start(f32[2,1,8,512]{3,2,1,0:T(8,128)S(1)} %get-tuple-element.128), channel_id=1, source_target_pairs={{4,0},{8,4},{12,8},{16,12},{20,16},{24,20},{28,24},{5,1},{9,5},{13... | collective-permute-start | bytes 98312 | tf_op jit(solution)/shard_map/ppermute | solution.py:19
  163.5 4.9 %collective-permute-start.10 = (f32[2,6,1,512]{3,2,1,0:T(1,128)S(1)}, f32[2,6,1,512]{3,2,1,0:T(1,128)S(1)}, u32[]{:S(2)}, u32[]{:S(2)}) collective-permute-start(f32[2,6,1,512]{3,2,1,0:T(1,128)S(1)} %get-tuple-element.123), channel_id=1, source_target_pairs={{0,1},{1,2},{2,3},{4,5},{5,6},{6,7},{8,9},{9,10},{10,11},{12,13},{... | collective-permute-start | bytes 73736 | tf_op jit(solution)/shard_map/ppermute | solution.py:17
  166.3 5.7 %collective-permute-start.11 = (f32[2,6,1,512]{3,2,1,0:T(1,128)S(1)}, f32[2,6,1,512]{3,2,1,0:T(1,128)S(1)}, u32[]{:S(2)}, u32[]{:S(2)}) collective-permute-start(f32[2,6,1,512]{3,2,1,0:T(1,128)S(1)} %get-tuple-element.124), channel_id=1, source_target_pairs={{1,0},{2,1},{3,2},{5,4},{6,5},{7,6},{9,8},{10,9},{11,10},{13,12},{... | collective-permute-start | bytes 73736 | tf_op jit(solution)/shard_map/ppermute | solution.py:19
  (90 other events, 77.1 us)
where the time goes:
time: 176 us; the launch traced here: 174 us
  starting transfers between devices  64 us (36%)
  local copies, waits for them, and re-layouts  48.9 us (28%)
  waiting for transfers between devices  39.7 us (23%)
  other arithmetic  17.7 us (10%)
  between operations  3.23 us (2%)
    unnamed x285, local copies, waits for them, and re-layouts  32.5 us
    ppermute x6, waiting for transfers between devices, with_halo(): lax.ppermute(head, axis, [((i + 1) % count, i) for i in range(ends)])  22.8 us
    ppermute x6, starting transfers between devices, with_halo(): lax.ppermute(tail, axis, [(i, (i + 1) % count) for i in range(ends)])  14.1 us
    all_to_all x2, starting transfers between devices, solve_rows_moved(): lax.all_to_all(source, 'row', split_axis=2, concat_axis=0, tiled=True)  10.4 us
    all_to_all x2, waiting for transfers between devices, along_lines(): lax.all_to_all(solved, 'col', split_axis=1, concat_axis=2, tiled=True)  8.33 us
    all_to_all x2, starting transfers between devices, along_lines(): lax.all_to_all(solved, 'col', split_axis=1, concat_axis=2, tiled=True)  8.02 us
    ppermute x6, starting transfers between devices, with_halo(): lax.ppermute(head, axis, [((i + 1) % count, i) for i in range(ends)])  7.75 us
    all_to_all x2, starting transfers between devices, along_lines(): lax.all_to_all(solved, 'row', split_axis=0, concat_axis=2, tiled=True)  7.32 us
  transfers between devices with their start and end apart: 22, of which 14 were waited for; matrix products, arithmetic and copies ran while one was open for 22% of the time, Pallas kernels for 0%

commit v1 on v0

--- a/solution.py
+++ b/solution.py
@@ -1,7 +1,434 @@
+import functools
+
 import jax
 import jax.numpy as jnp
 from jax import lax
+from jax.experimental import pallas as pl
+from jax.experimental.pallas import tpu as pltpu
 from jax.sharding import PartitionSpec as P
+
+STEP = 30.0
+MESH = pl.DeviceIdType.MESH
+SIDE = 15.0
+AREA = 900.0
+
+
+def roll_to(values, stride, axis):
+    return pltpu.roll(values, stride % values.shape[axis], axis)
+
+
+def edge(shape, axis, where_at):
+    return lax.broadcasted_iota(jnp.int32, shape, axis) == where_at
+
+
+def up_x(values):
+    last = edge(values.shape, 2, values.shape[2] - 1)
+    return jnp.where(last, 0.0, roll_to(values, -1, 2)) - values
+
+
+def down_x(values):
+    return values - jnp.where(edge(values.shape, 2, 0), 0.0, roll_to(values, 1, 2))
+
+
+def up_z(values, above):
+    last = edge(values.shape, 1, values.shape[1] - 1)
+    return jnp.where(last, above, roll_to(values, -1, 1)) - values
+
+
+def down_z(values, below):
+    return values - jnp.where(edge(values.shape, 1, 0), below, roll_to(values, 1, 1))
+
+
+def up_y(values, above):
+    return jnp.concatenate([values[1:], above], 0) - values
+
+
+def down_y(values, below):
+    return values - jnp.concatenate([below, values[:-1]], 0)
+
+
+def levels_of(length):
+    strides = []
+    while (1 << len(strides)) < length:
+        strides.append(1 << len(strides))
+    return strides
+
+
+def chain_factors(link, excess, axis, keep):
+    for level, stride in enumerate(levels_of(link.shape[axis])):
+        link_hi = roll_to(link, -stride, axis)
+        inverse = 1.0 / (link + link_hi + excess)
+        ratio_lo = link * roll_to(inverse, stride, axis)
+        ratio_hi = roll_to(link * inverse, -stride, axis)
+        keep(2 * level, ratio_lo)
+        keep(2 * level + 1, ratio_hi)
+        excess = (
+            excess
+            + ratio_lo * roll_to(excess, stride, axis)
+            + ratio_hi * roll_to(excess, -stride, axis)
+        )
+        link = ratio_lo * roll_to(link, stride, axis)
+    return 1.0 / excess
+
+
+def chain_solve(load, inverse, load_source, axis):
+    source = load_source
+    for level, stride in enumerate(levels_of(source.shape[axis])):
+        source = (
+            source
+            + load(2 * level) * roll_to(source, stride, axis)
+            + load(2 * level + 1) * roll_to(source, -stride, axis)
+        )
+    return source * inverse
+
+
+def kernel(
+    rows, cols,
+    ex, ey, ez, hx, hy, hz, eps, sig,
+    o_ex, o_ey, o_ez, o_hx, o_hy, o_hz,
+    y_mat, z_mat, y_mat_in, z_mat_in,
+    y_src, z_src, y_src_in, z_src_in,
+    y_out, z_out, y_back, z_back,
+    face_z, halo_y, halo_z,
+    y_alpha, y_beta, z_alpha, z_beta, z_fwd, z_bwd,
+    x_fac, y_fac, z_fac,
+    halo_sems, row_send, row_recv, col_send, col_recv,
+):
+    ny, nz, nx = ex.shape
+    r = lax.axis_index("row")
+    c = lax.axis_index("col")
+    zero_y = jnp.zeros(halo_y.shape, jnp.float32)
+    zero_z = jnp.zeros(halo_z.shape, jnp.float32)
+    halo_y[...] = zero_y
+    halo_z[...] = zero_z
+    barrier = pltpu.get_barrier_semaphore()
+    for d in range(1, rows):
+        pl.semaphore_signal(
+            barrier, inc=1, device_id=(lax.rem(r + d, rows), c), device_id_type=MESH
+        )
+    for d in range(1, cols):
+        pl.semaphore_signal(
+            barrier, inc=1, device_id=(r, lax.rem(c + d, cols)), device_id_type=MESH
+        )
+
+    def halo(number, source, target, device):
+        return pltpu.make_async_remote_copy(
+            src_ref=source, dst_ref=target,
+            send_sem=halo_sems.at[0, number], recv_sem=halo_sems.at[1, number],
+            device_id=device, device_id_type=MESH,
+        )
+
+    face_z[0] = ex[:, 0:1, :]
+    face_z[1] = hy[:, nz - 1 : nz, :]
+    low_r, high_r = jnp.maximum(r - 1, 0), jnp.minimum(r + 1, rows - 1)
+    low_c, high_c = jnp.maximum(c - 1, 0), jnp.minimum(c + 1, cols - 1)
+    halos = [
+        (r > 0, r < rows - 1, halo(0, ez.at[0], halo_y.at[0], (low_r, c))),
+        (c < cols - 1, c > 0, halo(1, face_z.at[1], halo_z.at[1], (r, high_c))),
+        (r < rows - 1, r > 0, halo(2, hx.at[ny - 1], halo_y.at[1], (high_r, c))),
+        (c > 0, c < cols - 1, halo(3, face_z.at[0], halo_z.at[0], (r, low_c))),
+    ]
+
+    def start_halos():
+        for target, _, copy in halos:
+            pl.when(target)(copy.start)
+
+    def wait_halo(number):
+        target, sender, copy = halos[number]
+        pl.when(sender)(copy.wait_recv)
+
+    sent = []
+
+    def exchange(step, axis, source, target):
+        if axis == "row":
+            count, me, send, recv = rows, r, row_send, row_recv
+        else:
+            count, me, send, recv = cols, c, col_send, col_recv
+        copies = []
+        for d in range(1, count):
+            peer = lax.rem(me + d, count)
+            copies.append(
+                pltpu.make_async_remote_copy(
+                    src_ref=source.at[peer], dst_ref=target.at[me],
+                    send_sem=send.at[step, d - 1], recv_sem=recv.at[step, d - 1],
+                    device_id=(peer, c) if axis == "row" else (r, peer),
+                    device_id_type=MESH,
+                )
+            )
+        for copy in copies:
+            copy.start()
+        target[me] = source[me]
+        sent.extend(copies)
+        return copies
+
+    def arrive(copies):
+        for copy in copies:
+            copy.wait_recv()
+
+    pl.semaphore_wait(barrier, rows - 1 + cols - 1)
+    start_halos()
+
+    ground = (eps[...] + SIDE * sig[...]) * (1.0 / AREA)
+    link = jnp.ones((nz, nx), jnp.float32)
+    left = ground[0]
+    carry = ground[1] * 0.0
+    for j in range(1, ny):
+        here = ground[j] + carry
+        beta = 1.0 / (link + 1.0 + here)
+        alpha = link * beta
+        y_alpha[j] = alpha
+        y_beta[j] = beta
+        left = left + alpha * here
+        carry = beta * here
+        link = alpha
+    for p in range(rows):
+        y_mat[p, 0:1, :] = link[p : p + 1]
+        y_mat[p, 1:2, :] = left[p : p + 1]
+        y_mat[p, 2:3, :] = carry[p : p + 1]
+    y_mat_copies = exchange(0, "row", y_mat, y_mat_in)
+
+    spot = lax.broadcasted_iota(jnp.int32, (ny, nz, nx), 1)
+    here = ground
+    link = jnp.ones((ny, nz, nx), jnp.float32)
+    beta = jnp.ones((ny, nz, nx), jnp.float32)
+    for j in range(1, nz):
+        flow = beta * here if j > 1 else jnp.zeros_like(here)
+        fresh_link = link if j == 1 else roll_to(link * beta, 1, 1)
+        fresh = ground + roll_to(flow, 1, 1)
+        here = jnp.where(spot == j, fresh, here)
+        link = jnp.where(spot == j, fresh_link, link)
+        beta = jnp.where(spot == j, 1.0 / (link + 1.0 + here), beta)
+    first = spot == 0
+    beta = jnp.where(first, 0.0, beta)
+    alpha = link * beta
+    z_alpha[...] = alpha
+    z_beta[...] = beta
+    left = jnp.sum(jnp.where(first, ground, alpha * here), axis=1)
+    tail = beta * here
+    for p in range(cols):
+        z_mat[p, 0:1, :] = alpha[p, nz - 1 :, :]
+        z_mat[p, 1:2, :] = left[p : p + 1]
+        z_mat[p, 2:3, :] = tail[p, nz - 1 :, :]
+    z_mat_copies = exchange(0, "col", z_mat, z_mat_in)
+    forward = jnp.where(first, 0.0, roll_to(beta, 1, 1))
+    backward = jnp.where(spot == nz - 1, 0.0, beta)
+    for level, stride in enumerate(levels_of(nz)):
+        z_fwd[level] = forward
+        z_bwd[level] = backward
+        forward = forward * jnp.where(spot < stride, 0.0, roll_to(forward, stride, 1))
+        backward = backward * jnp.where(
+            spot >= nz - stride, 0.0, roll_to(backward, -stride, 1)
+        )
+
+    def reduce_y(body, flux):
+        charge = []
+        left = body[0] + flux[0]
+        for j in range(1, ny):
+            now = body[j] + flux[j] - flux[j - 1]
+            if j > 1:
+                now = now + y_beta[j - 1] * charge[-1]
+            charge.append(now)
+            left = left + y_alpha[j] * now
+        right = y_beta[ny - 1] * charge[-1] - flux[ny - 1]
+        return charge, left, right
+
+    def send_y(stage, left, right):
+        for p in range(rows):
+            y_src[stage, p, 0:1, :] = left[p : p + 1]
+            y_src[stage, p, 1:2, :] = right[p : p + 1]
+        return exchange(1 + 2 * stage, "row", y_src.at[stage], y_src_in.at[stage])
+
+    def expand_y(stage, charge):
+        near = jnp.concatenate([y_back[stage, p, 0:1, :] for p in range(rows)], 0)
+        beyond = jnp.concatenate([y_back[stage, p, 1:2, :] for p in range(rows)], 0)
+        cells = []
+        after = beyond
+        for j in range(ny - 1, 0, -1):
+            after = y_alpha[j] * near + y_beta[j] * (after + charge[j - 1])
+            cells.insert(0, after)
+        return jnp.stack([near] + cells, 0), beyond[None]
+
+    def reduce_z(body, flux):
+        source = body + flux - jnp.where(first, 0.0, roll_to(flux, 1, 1))
+        charge = jnp.where(first, 0.0, source)
+        for level, stride in enumerate(levels_of(nz)):
+            charge = charge + z_fwd[level] * roll_to(charge, stride, 1)
+        left = jnp.sum(jnp.where(first, source, z_alpha[...] * charge), axis=1)
+        right = z_beta[...] * charge - flux
+        return charge, left, right
+
+    def send_z(stage, left, right):
+        for p in range(cols):
+            z_src[stage, p, 0:1, :] = left[p : p + 1]
+            z_src[stage, p, 1:2, :] = right[p, nz - 1 :, :]
+        return exchange(1 + 2 * stage, "col", z_src.at[stage], z_src_in.at[stage])
+
+    def expand_z(stage, charge):
+        near = jnp.stack([z_back[stage, p, 0:1, :] for p in range(cols)], 0)
+        beyond = jnp.stack([z_back[stage, p, 1:2, :] for p in range(cols)], 0)
+        cells = z_alpha[...] * near + z_beta[...] * charge
+        cells = cells + jnp.where(spot == nz - 1, z_beta[...] * beyond, 0.0)
+        cells = jnp.where(first, near, cells)
+        for level, stride in enumerate(levels_of(nz)):
+            cells = cells + z_bwd[level] * roll_to(cells, -stride, 1)
+        return cells, beyond
+
+    tall = 8
+
+    def rows_of(buffer, number, count, filler):
+        parts = [buffer[p, number : number + 1, :] for p in range(count)]
+        if count < tall:
+            parts.append(jnp.full((tall - count, nx), filler, jnp.float32))
+        return jnp.concatenate(parts, 0)
+
+    def line_factors(buffer, count, keep):
+        row = lax.broadcasted_iota(jnp.int32, (tall, nx), 0)
+        link = rows_of(buffer, 0, count, 0.0)
+        left = rows_of(buffer, 1, count, 1.0)
+        right = rows_of(buffer, 2, count, 0.0)
+        below = row == 0
+        excess = left + jnp.where(below, 0.0, roll_to(right, 1, 0))
+        excess = excess + jnp.where(row == count - 1, link, 0.0)
+        inner_link = jnp.where(below | (row >= count), 0.0, roll_to(link, 1, 0))
+        return chain_factors(inner_link, excess, 0, keep)
+
+    def line_solve(stage, source_in, count, load, inverse, out):
+        row = lax.broadcasted_iota(jnp.int32, (tall, nx), 0)
+        left = rows_of(source_in.at[stage], 0, count, 0.0)
+        right = rows_of(source_in.at[stage], 1, count, 0.0)
+        source = left + jnp.where(row == 0, 0.0, roll_to(right, 1, 0))
+        source = jnp.where(row < count, source, 0.0)
+        near = chain_solve(load, inverse, source, 0)
+        for p in range(count):
+            out[stage, p, 0:1, :] = near[p : p + 1]
+            if p < count - 1:
+                out[stage, p, 1:2, :] = near[p + 1 : p + 2]
+            else:
+                out[stage, p, 1:2, :] = jnp.zeros((1, nx), jnp.float32)
+
+    def keeper(ref):
+        def keep(number, values):
+            ref[number] = values
+        return keep
+
+    def loader(ref):
+        def load(number):
+            return ref[number]
+        return load
+
+    keep_ground = (eps[...] - SIDE * sig[...]) * (1.0 / AREA)
+    flux_of_z = hz[...] * (1.0 / STEP) - up_x(ey[...])
+    wait_halo(1)
+    body = keep_ground * ex[...] - down_z(hy[...], halo_z[1]) * (1.0 / STEP)
+    y_charge, left, right = reduce_y(body, flux_of_z)
+    y_copies = send_y(0, left, right)
+    wait_halo(0)
+    flux_of_x = hx[...] * (1.0 / STEP) - up_y(ez[...], halo_y[0:1])
+    body = keep_ground * ey[...] - down_x(hz[...]) * (1.0 / STEP)
+    z_charge, left, right = reduce_z(body, flux_of_x)
+    z_copies = send_z(0, left, right)
+
+    arrive(y_mat_copies)
+    y_inverse = line_factors(y_mat_in, rows, keeper(y_fac))
+    arrive(z_mat_copies)
+    z_inverse = line_factors(z_mat_in, cols, keeper(z_fac))
+
+    def half_lines(stage, y_copies, z_copies):
+        arrive(y_copies)
+        line_solve(stage, y_src_in, rows, loader(y_fac), y_inverse, y_out)
+        y_returns = exchange(2 + 2 * stage, "row", y_out.at[stage], y_back.at[stage])
+        arrive(z_copies)
+        line_solve(stage, z_src_in, cols, loader(z_fac), z_inverse, z_out)
+        z_returns = exchange(2 + 2 * stage, "col", z_out.at[stage], z_back.at[stage])
+        return y_returns, z_returns
+
+    y_returns, z_returns = half_lines(0, y_copies, z_copies)
+
+    first_x = lax.broadcasted_iota(jnp.int32, (ny, nz, nx), 2) == 0
+    last_x = lax.broadcasted_iota(jnp.int32, (ny, nz, nx), 2) == nx - 1
+    x_inverse = chain_factors(
+        jnp.where(first_x, 0.0, 1.0), ground + jnp.where(last_x, 1.0, 0.0), 2, keeper(x_fac)
+    )
+    wait_halo(2)
+    wait_halo(3)
+    flux_of_y = hy[...] * (1.0 / STEP) - up_z(ex[...], halo_z[0])
+    body = keep_ground * ez[...] - down_y(hx[...], halo_y[1:2]) * (1.0 / STEP)
+    half_ez = chain_solve(loader(x_fac), x_inverse, body + down_x(flux_of_y), 2)
+    slope_ez = up_x(half_ez)
+
+    arrive(y_returns)
+    half_ex, beyond_ex = expand_y(0, y_charge)
+    slope_ex = up_y(half_ex, beyond_ex)
+    arrive(z_returns)
+    half_ey, beyond_ey = expand_z(0, z_charge)
+    slope_ey = up_z(half_ey, beyond_ey)
+
+    lossless = eps[...] * (1.0 / AREA)
+    lossy = sig[...] * (SIDE / AREA)
+    y_charge, left, right = reduce_y(lossless * half_ez + lossy * ez[...], -slope_ey)
+    y_copies = send_y(1, left, right)
+    z_charge, left, right = reduce_z(lossless * half_ex + lossy * ex[...], -slope_ez)
+    z_copies = send_z(1, left, right)
+    y_returns, z_returns = half_lines(1, y_copies, z_copies)
+
+    body = lossless * half_ey + lossy * ey[...]
+    mean_ey = chain_solve(loader(x_fac), x_inverse, body - down_x(slope_ex), 2)
+    next_ey = 2.0 * mean_ey - ey[...]
+    o_ey[...] = next_ey
+    o_hz[...] = STEP * (flux_of_z + 2.0 * slope_ex - up_x(next_ey))
+
+    arrive(y_returns)
+    mean_ez, beyond_ez = expand_y(1, y_charge)
+    next_ez = 2.0 * mean_ez - ez[...]
+    o_ez[...] = next_ez
+    above = 2.0 * beyond_ez - halo_y[0:1]
+    o_hx[...] = STEP * (flux_of_x + 2.0 * slope_ey - up_y(next_ez, above))
+    arrive(z_returns)
+    mean_ex, beyond_ex = expand_z(1, z_charge)
+    next_ex = 2.0 * mean_ex - ex[...]
+    o_ex[...] = next_ex
+    above = 2.0 * beyond_ex - halo_z[0]
+    o_hy[...] = STEP * (flux_of_y + 2.0 * slope_ez - up_z(next_ex, above))
+
+    for target, _, copy in halos:
+        pl.when(target)(copy.wait_send)
+    for copy in sent:
+        copy.wait_send()
+
+
+def fused(rows, cols, *fields):
+    ny, nz, nx = fields[0].shape
+    f32 = jnp.float32
+    block = (ny, nz, nx)
+    y_levels, z_levels = len(levels_of(8)), len(levels_of(8))
+    scratch = [
+        (rows, 3, nx), (cols, 3, nx), (rows, 3, nx), (cols, 3, nx),
+        (2, rows, 2, nx), (2, cols, 2, nx), (2, rows, 2, nx), (2, cols, 2, nx),
+        (2, rows, 2, nx), (2, cols, 2, nx), (2, rows, 2, nx), (2, cols, 2, nx),
+        (2, ny, 1, nx), (2, nz, nx), (2, ny, 1, nx),
+        block, block, block, block,
+        (len(levels_of(nz)),) + block, (len(levels_of(nz)),) + block,
+        (2 * len(levels_of(nx)),) + block, (2 * y_levels, 8, nx), (2 * z_levels, 8, nx),
+    ]
+    return pl.pallas_call(
+        functools.partial(kernel, rows, cols),
+        out_shape=[jax.ShapeDtypeStruct(block, f32)] * 6,
+        in_specs=[pl.BlockSpec(memory_space=pltpu.VMEM)] * 8,
+        out_specs=[pl.BlockSpec(memory_space=pltpu.VMEM)] * 6,
+        scratch_shapes=[pltpu.VMEM(shape, f32) for shape in scratch]
+        + [
+            pltpu.SemaphoreType.DMA((2, 4)),
+            pltpu.SemaphoreType.DMA((5, rows - 1)),
+            pltpu.SemaphoreType.DMA((5, rows - 1)),
+            pltpu.SemaphoreType.DMA((5, cols - 1)),
+            pltpu.SemaphoreType.DMA((5, cols - 1)),
+        ],
+        compiler_params=pltpu.CompilerParams(
+            collective_id=0, has_side_effects=True, vmem_limit_bytes=40 * 1024 * 1024
+        ),
+        name="step",
+    )(*fields)
+
 
 HALF_STEP = 30.0
 
@@ -215,6 +642,7 @@
 
 
 def solution(mesh):
+    rows, cols = mesh.shape["row"], mesh.shape["col"]
     placed = (
         P("row", "col", None),
         P("row", "col", None),
@@ -225,8 +653,15 @@
         P("row", "col", None),
         P("row", "col", None),
     )
+
+    def per_device(*fields):
+        ny, nz = fields[0].shape[:2]
+        if nz == rows == 8 and ny == cols and 1 < cols < 8:
+            return tuple(fused(rows, cols, *fields))
+        return on_device(*fields)
+
     return jax.shard_map(
-        on_device,
+        per_device,
         mesh=mesh,
         in_specs=placed,
         out_specs=(

time: 176 us -> 34.8 us (0.20); the launches traced: 174 us -> 34.3 us
  starting transfers between devices: 64 us -> 0 us
  waiting for transfers between devices: 39.7 us -> 0 us
  local copies, waits for them, and re-layouts: 48.9 us -> 10.5 us
  Pallas kernels: 0 us -> 23.2 us
  other arithmetic: 17.7 us -> 0 us
  between operations: 3.23 us -> 0.66 us
    all_to_all x10 -> x0, starting transfers between devices: 42.2 us -> none  [the longest x2 10.4 us: solve_rows_moved(): lax.all_to_all(source, 'row', split_axis=2, concat_axis=0, tiled=True)]
    ppermute x12 -> x0, waiting for transfers between devices: 23.4 us -> none  [the longest x6 22.8 us: with_halo(): lax.ppermute(head, axis, [((i + 1) % count, i) for i in range(ends)])]
    pallas_call x0 -> x1, Pallas kernels: none -> 23.2 us  [fused(): pl.pallas_call(functools.partial(kernel, rows, cols), out_shape=[jax.Shap...]
    unnamed x285 -> x22, local copies, waits for them, and re-layouts: 32.5 us -> 10.5 us
    ppermute x12 -> x0, starting transfers between devices: 21.8 us -> none  [the longest x6 14.1 us: with_halo(): lax.ppermute(tail, axis, [(i, (i + 1) % count) for i in range(ends)])]
    all_to_all x10 -> x0, waiting for transfers between devices: 16.3 us -> none  [the longest x2 8.33 us: along_lines(): lax.all_to_all(solved, 'col', split_axis=1, concat_axis=2, tiled=True)]
    slice x108 -> x0, local copies, waits for them, and re-layouts: 7.89 us -> none  [the longest x64 4.77 us: shifted(): lax.slice_in_dim(values, 0, length - stride, axis=line_axis)]
    all_to_all x8 -> x0, other arithmetic: 7.17 us -> none  [the longest x2 2.41 us: along_lines(): lax.all_to_all(solved, 'row', split_axis=0, concat_axis=2, tiled=True)]
  transfers between devices with their start and end apart: 22 -> 0, of which waited for: 14 -> 0; matrix products, arithmetic and copies ran while one was open for 22% -> 0% of each run, Pallas kernels for 0% -> 0%
where the time goes in v1:
time: 34.8 us; the launch traced here: 34.3 us
  Pallas kernels  23.2 us (67%)
  local copies, waits for them, and re-layouts  10.5 us (30%)
  between operations  0.66 us (2%)
    pallas_call x1, Pallas kernels, fused(): pl.pallas_call(functools.partial(kernel, rows, cols), out_shape=[jax.Shap...  23.2 us
    unnamed x22, local copies, waits for them, and re-layouts  10.5 us

profile of v1, /device:TPU:0, one launch (start us, length us, event | category | flops | bytes accessed | tf_op | source)
XLA Modules:
  0.0 34.3 jit_solution(6178127686426714721)
XLA Ops:
  0.6 0.0 copy-start
  0.6 0.8 %copy-done = f32[4,8,512]{2,1,0:T(8,128)S(1)} copy-done((f32[4,8,512]{2,1,0:T(8,128)S(1)}, f32[4,8,512]{2,1,0:T(8,128)}, u32[]{:S(2)}) %copy-start) | copy-done | bytes 65560
  1.5 0.0 copy-start.1
  1.5 0.8 %copy-done.1 = f32[4,8,512]{2,1,0:T(8,128)S(1)} copy-done((f32[4,8,512]{2,1,0:T(8,128)S(1)}, f32[4,8,512]{2,1,0:T(8,128)}, u32[]{:S(2)}) %copy-start.1) | copy-done | bytes 65560
  2.3 0.0 copy-start.2
  2.3 0.8 %copy-done.2 = f32[4,8,512]{2,1,0:T(8,128)S(1)} copy-done((f32[4,8,512]{2,1,0:T(8,128)S(1)}, f32[4,8,512]{2,1,0:T(8,128)}, u32[]{:S(2)}) %copy-start.2) | copy-done | bytes 65560
  3.2 0.0 copy-start.3
  3.2 0.8 %copy-done.3 = f32[4,8,512]{2,1,0:T(8,128)S(1)} copy-done((f32[4,8,512]{2,1,0:T(8,128)S(1)}, f32[4,8,512]{2,1,0:T(8,128)}, u32[]{:S(2)}) %copy-start.3) | copy-done | bytes 65560
  4.0 0.0 copy-start.4
  4.0 0.8 %copy-done.4 = f32[4,8,512]{2,1,0:T(8,128)S(1)} copy-done((f32[4,8,512]{2,1,0:T(8,128)S(1)}, f32[4,8,512]{2,1,0:T(8,128)}, u32[]{:S(2)}) %copy-start.4) | copy-done | bytes 65560
  4.8 0.0 copy-start.5
  4.8 0.8 %copy-done.5 = f32[4,8,512]{2,1,0:T(8,128)S(1)} copy-done((f32[4,8,512]{2,1,0:T(8,128)S(1)}, f32[4,8,512]{2,1,0:T(8,128)}, u32[]{:S(2)}) %copy-start.5) | copy-done | bytes 65560
  5.7 0.0 copy-start.6
  5.7 0.8 %copy-done.6 = f32[4,8,512]{2,1,0:T(8,128)S(1)} copy-done((f32[4,8,512]{2,1,0:T(8,128)S(1)}, f32[4,8,512]{2,1,0:T(8,128)}, u32[]{:S(2)}) %copy-start.6) | copy-done | bytes 65560
  6.5 0.0 copy-start.7
  6.5 0.8 %copy-done.7 = f32[4,8,512]{2,1,0:T(8,128)S(1)} copy-done((f32[4,8,512]{2,1,0:T(8,128)S(1)}, f32[4,8,512]{2,1,0:T(8,128)}, u32[]{:S(2)}) %copy-start.7) | copy-done | bytes 65560
  7.4 23.2 %step.1 = (f32[4,8,512]{2,1,0:T(8,128)S(1)}, f32[4,8,512]{2,1,0:T(8,128)S(1)}, f32[4,8,512]{2,1,0:T(8,128)S(1)}, f32[4,8,512]{2,1,0:T(8,128)S(1)}, f32[4,8,512]{2,1,0:T(8,128)S(1)}, /*index=5*/f32[4,8,512]{2,1,0:T(8,128)S(1)}) custom-call(f32[4,8,512]{2,1,0:T(8,128)S(1)} %copy-done, f32[4,8,512]{2,1,0:T(8,128)S(1)} %copy-done.1, f32[4,8,512]{2,1,0:T(8,128)S(1)} %copy-done.2, ...), custom_call_target="tpu_custom_call" | custom-call | tf_op jit(solution)/shard_map/step/pallas_call | solution.py:413
  30.5 0.6 %copy.20 = f32[4,8,512]{2,1,0:T(8,128)} copy(f32[4,8,512]{2,1,0:T(8,128)S(1)} %get-tuple-element.12) | data formatting | bytes 131072
  31.1 0.6 %copy.21 = f32[4,8,512]{2,1,0:T(8,128)} copy(f32[4,8,512]{2,1,0:T(8,128)S(1)} %get-tuple-element.13) | data formatting | bytes 131072
  31.8 0.6 %copy.22 = f32[4,8,512]{2,1,0:T(8,128)} copy(f32[4,8,512]{2,1,0:T(8,128)S(1)} %get-tuple-element.14) | data formatting | bytes 131072
  32.4 0.6 %copy.23 = f32[4,8,512]{2,1,0:T(8,128)} copy(f32[4,8,512]{2,1,0:T(8,128)S(1)} %get-tuple-element.15) | data formatting | bytes 131072
  33.0 0.6 %copy.24 = f32[4,8,512]{2,1,0:T(8,128)} copy(f32[4,8,512]{2,1,0:T(8,128)S(1)} %get-tuple-element.16) | data formatting | bytes 131072
  33.7 0.6 %copy.25 = f32[4,8,512]{2,1,0:T(8,128)} copy(f32[4,8,512]{2,1,0:T(8,128)S(1)} %get-tuple-element.17) | data formatting | bytes 131072
Async XLA Ops:
  0.6 0.8 %copy-start = (f32[4,8,512]{2,1,0:T(8,128)S(1)}, f32[4,8,512]{2,1,0:T(8,128)}, u32[]{:S(2)}) copy-start(f32[4,8,512]{2,1,0:T(8,128)} %ex.1) | copy-start | bytes 196612
  1.5 0.8 %copy-start.1 = (f32[4,8,512]{2,1,0:T(8,128)S(1)}, f32[4,8,512]{2,1,0:T(8,128)}, u32[]{:S(2)}) copy-start(f32[4,8,512]{2,1,0:T(8,128)} %ey.1) | copy-start | bytes 196612
  2.3 0.8 %copy-start.2 = (f32[4,8,512]{2,1,0:T(8,128)S(1)}, f32[4,8,512]{2,1,0:T(8,128)}, u32[]{:S(2)}) copy-start(f32[4,8,512]{2,1,0:T(8,128)} %ez.1) | copy-start | bytes 196612
  3.2 0.8 %copy-start.3 = (f32[4,8,512]{2,1,0:T(8,128)S(1)}, f32[4,8,512]{2,1,0:T(8,128)}, u32[]{:S(2)}) copy-start(f32[4,8,512]{2,1,0:T(8,128)} %hx.1) | copy-start | bytes 196612
  4.0 0.8 %copy-start.4 = (f32[4,8,512]{2,1,0:T(8,128)S(1)}, f32[4,8,512]{2,1,0:T(8,128)}, u32[]{:S(2)}) copy-start(f32[4,8,512]{2,1,0:T(8,128)} %hy.1) | copy-start | bytes 196612
  4.8 0.8 %copy-start.5 = (f32[4,8,512]{2,1,0:T(8,128)S(1)}, f32[4,8,512]{2,1,0:T(8,128)}, u32[]{:S(2)}) copy-start(f32[4,8,512]{2,1,0:T(8,128)} %hz.1) | copy-start | bytes 196612
  5.7 0.8 %copy-start.6 = (f32[4,8,512]{2,1,0:T(8,128)S(1)}, f32[4,8,512]{2,1,0:T(8,128)}, u32[]{:S(2)}) copy-start(f32[4,8,512]{2,1,0:T(8,128)} %eps.1) | copy-start | bytes 196612
  6.5 0.8 %copy-start.7 = (f32[4,8,512]{2,1,0:T(8,128)S(1)}, f32[4,8,512]{2,1,0:T(8,128)}, u32[]{:S(2)}) copy-start(f32[4,8,512]{2,1,0:T(8,128)} %sig.1) | copy-start | bytes 196612

commit v2 on v1

--- a/solution.py
+++ b/solution.py
@@ -10,6 +10,7 @@
 STEP = 30.0
 MESH = pl.DeviceIdType.MESH
 SIDE = 15.0
+VMEM_LIMIT = 40 * 1024 * 1024
 AREA = 900.0
 
 
@@ -84,7 +85,10 @@
 
 def kernel(
     rows, cols,
-    ex, ey, ez, hx, hy, hz, eps, sig,
+    *refs,
+):
+    hbm = refs[:8]
+    (
     o_ex, o_ey, o_ez, o_hx, o_hy, o_hz,
     y_mat, z_mat, y_mat_in, z_mat_in,
     y_src, z_src, y_src_in, z_src_in,
@@ -93,7 +97,14 @@
     y_alpha, y_beta, z_alpha, z_beta, z_fwd, z_bwd,
     x_fac, y_fac, z_fac,
     halo_sems, row_send, row_recv, col_send, col_recv,
-):
+    fields, field_sems,
+    ) = refs[8:]
+    ex, ey, ez, hx, hy, hz, eps, sig = [fields.at[i] for i in range(8)]
+    loads = [
+        pltpu.make_async_copy(hbm[i], fields.at[i], field_sems.at[i]) for i in range(8)
+    ]
+    for i in (6, 7, 0, 4, 2, 3, 5, 1):
+        loads[i].start()
     ny, nz, nx = ex.shape
     r = lax.axis_index("row")
     c = lax.axis_index("col")
@@ -118,8 +129,6 @@
             device_id=device, device_id_type=MESH,
         )
 
-    face_z[0] = ex[:, 0:1, :]
-    face_z[1] = hy[:, nz - 1 : nz, :]
     low_r, high_r = jnp.maximum(r - 1, 0), jnp.minimum(r + 1, rows - 1)
     low_c, high_c = jnp.maximum(c - 1, 0), jnp.minimum(c + 1, cols - 1)
     halos = [
@@ -165,9 +174,8 @@
         for copy in copies:
             copy.wait_recv()
 
-    pl.semaphore_wait(barrier, rows - 1 + cols - 1)
-    start_halos()
-
+    loads[6].wait()
+    loads[7].wait()
     ground = (eps[...] + SIDE * sig[...]) * (1.0 / AREA)
     link = jnp.ones((nz, nx), jnp.float32)
     left = ground[0]
@@ -185,6 +193,12 @@
         y_mat[p, 0:1, :] = link[p : p + 1]
         y_mat[p, 1:2, :] = left[p : p + 1]
         y_mat[p, 2:3, :] = carry[p : p + 1]
+    for i in (0, 4, 2, 3):
+        loads[i].wait()
+    face_z[0] = ex[:, 0:1, :]
+    face_z[1] = hy[:, nz - 1 : nz, :]
+    pl.semaphore_wait(barrier, rows - 1 + cols - 1)
+    start_halos()
     y_mat_copies = exchange(0, "row", y_mat, y_mat_in)
 
     spot = lax.broadcasted_iota(jnp.int32, (ny, nz, nx), 1)
@@ -316,6 +330,14 @@
             return ref[number]
         return load
 
+    first_x = lax.broadcasted_iota(jnp.int32, (ny, nz, nx), 2) == 0
+    last_x = lax.broadcasted_iota(jnp.int32, (ny, nz, nx), 2) == nx - 1
+    x_inverse = chain_factors(
+        jnp.where(first_x, 0.0, 1.0), ground + jnp.where(last_x, 1.0, 0.0), 2, keeper(x_fac)
+    )
+
+    loads[5].wait()
+    loads[1].wait()
     keep_ground = (eps[...] - SIDE * sig[...]) * (1.0 / AREA)
     flux_of_z = hz[...] * (1.0 / STEP) - up_x(ey[...])
     wait_halo(1)
@@ -328,6 +350,13 @@
     z_charge, left, right = reduce_z(body, flux_of_x)
     z_copies = send_z(0, left, right)
 
+    wait_halo(2)
+    wait_halo(3)
+    flux_of_y = hy[...] * (1.0 / STEP) - up_z(ex[...], halo_z[0])
+    body = keep_ground * ez[...] - down_y(hx[...], halo_y[1:2]) * (1.0 / STEP)
+    half_ez = chain_solve(loader(x_fac), x_inverse, body + down_x(flux_of_y), 2)
+    slope_ez = up_x(half_ez)
+
     arrive(y_mat_copies)
     y_inverse = line_factors(y_mat_in, rows, keeper(y_fac))
     arrive(z_mat_copies)
@@ -344,18 +373,6 @@
 
     y_returns, z_returns = half_lines(0, y_copies, z_copies)
 
-    first_x = lax.broadcasted_iota(jnp.int32, (ny, nz, nx), 2) == 0
-    last_x = lax.broadcasted_iota(jnp.int32, (ny, nz, nx), 2) == nx - 1
-    x_inverse = chain_factors(
-        jnp.where(first_x, 0.0, 1.0), ground + jnp.where(last_x, 1.0, 0.0), 2, keeper(x_fac)
-    )
-    wait_halo(2)
-    wait_halo(3)
-    flux_of_y = hy[...] * (1.0 / STEP) - up_z(ex[...], halo_z[0])
-    body = keep_ground * ez[...] - down_y(hx[...], halo_y[1:2]) * (1.0 / STEP)
-    half_ez = chain_solve(loader(x_fac), x_inverse, body + down_x(flux_of_y), 2)
-    slope_ez = up_x(half_ez)
-
     arrive(y_returns)
     half_ex, beyond_ex = expand_y(0, y_charge)
     slope_ex = up_y(half_ex, beyond_ex)
@@ -369,11 +386,10 @@
     y_copies = send_y(1, left, right)
     z_charge, left, right = reduce_z(lossless * half_ex + lossy * ex[...], -slope_ez)
     z_copies = send_z(1, left, right)
-    y_returns, z_returns = half_lines(1, y_copies, z_copies)
-
     body = lossless * half_ey + lossy * ey[...]
     mean_ey = chain_solve(loader(x_fac), x_inverse, body - down_x(slope_ex), 2)
     next_ey = 2.0 * mean_ey - ey[...]
+    y_returns, z_returns = half_lines(1, y_copies, z_copies)
     o_ey[...] = next_ey
     o_hz[...] = STEP * (flux_of_z + 2.0 * slope_ex - up_x(next_ey))
 
@@ -394,6 +410,17 @@
         pl.when(target)(copy.wait_send)
     for copy in sent:
         copy.wait_send()
+
+
+def deliver(*refs):
+    held, results, sems = refs[:6], refs[6:12], refs[12]
+    copies = [
+        pltpu.make_async_copy(held[i], results[i], sems.at[i]) for i in range(6)
+    ]
+    for copy in copies:
+        copy.start()
+    for copy in copies:
+        copy.wait()
 
 
 def fused(rows, cols, *fields):
@@ -410,10 +437,10 @@
         (len(levels_of(nz)),) + block, (len(levels_of(nz)),) + block,
         (2 * len(levels_of(nx)),) + block, (2 * y_levels, 8, nx), (2 * z_levels, 8, nx),
     ]
-    return pl.pallas_call(
+    held = pl.pallas_call(
         functools.partial(kernel, rows, cols),
-        out_shape=[jax.ShapeDtypeStruct(block, f32)] * 6,
-        in_specs=[pl.BlockSpec(memory_space=pltpu.VMEM)] * 8,
+        out_shape=[pltpu.VMEM(block, f32)] * 6,
+        in_specs=[pl.BlockSpec(memory_space=pl.ANY)] * 8,
         out_specs=[pl.BlockSpec(memory_space=pltpu.VMEM)] * 6,
         scratch_shapes=[pltpu.VMEM(shape, f32) for shape in scratch]
         + [
@@ -422,12 +449,23 @@
             pltpu.SemaphoreType.DMA((5, rows - 1)),
             pltpu.SemaphoreType.DMA((5, cols - 1)),
             pltpu.SemaphoreType.DMA((5, cols - 1)),
+            pltpu.VMEM((8,) + block, f32),
+            pltpu.SemaphoreType.DMA((8,)),
         ],
         compiler_params=pltpu.CompilerParams(
-            collective_id=0, has_side_effects=True, vmem_limit_bytes=40 * 1024 * 1024
+            collective_id=0, has_side_effects=True, vmem_limit_bytes=VMEM_LIMIT
         ),
         name="step",
-    )(*fields)
+    )(*[pltpu.with_memory_space_constraint(field, pltpu.HBM) for field in fields])
+    return pl.pallas_call(
+        deliver,
+        out_shape=[jax.ShapeDtypeStruct(block, f32)] * 6,
+        in_specs=[pl.BlockSpec(memory_space=pltpu.VMEM)] * 6,
+        out_specs=[pl.BlockSpec(memory_space=pl.ANY)] * 6,
+        scratch_shapes=[pltpu.SemaphoreType.DMA((6,))],
+        compiler_params=pltpu.CompilerParams(vmem_limit_bytes=1024 * 1024),
+        name="deliver",
+    )(*held)
 
 
 HALF_STEP = 30.0

time: 34.8 us -> 24.9 us (0.72)
  local copies, waits for them, and re-layouts: 10.5 us -> 0 us
  Pallas kernels: 23.2 us -> 24.1 us
    unnamed x22 -> x0, local copies, waits for them, and re-layouts: 10.5 us -> none
    pallas_call x1 -> x2, Pallas kernels: 23.2 us -> 24.1 us  [the longest x1 23.3 us: fused(): pl.pallas_call(functools.partial(kernel, rows, cols), out_shape=[pltpu.VM...]
where the time goes in v2:
time: 24.9 us; the launch traced here: 24.7 us
  Pallas kernels  24.1 us (97%)
  between operations  0.64 us (3%)
    pallas_call x1, Pallas kernels, fused(): pl.pallas_call(functools.partial(kernel, rows, cols), out_shape=[pltpu.VM...  23.3 us
    pallas_call x1, Pallas kernels, fused(): pl.pallas_call(deliver, out_shape=[jax.ShapeDtypeStruct(block, f32)] * 6,...  0.79 us

profile of v2, /device:TPU:0, one launch (start us, length us, event | category | flops | bytes accessed | tf_op | source)
XLA Modules:
  0.0 24.7 jit_solution(10571963460535832672)
XLA Ops:
  0.6 23.3 %step.1 = (f32[4,8,512]{2,1,0:T(8,128)S(1)}, f32[4,8,512]{2,1,0:T(8,128)S(1)}, f32[4,8,512]{2,1,0:T(8,128)S(1)}, f32[4,8,512]{2,1,0:T(8,128)S(1)}, f32[4,8,512]{2,1,0:T(8,128)S(1)}, /*index=5*/f32[4,8,512]{2,1,0:T(8,128)S(1)}) custom-call(f32[4,8,512]{2,1,0:T(8,128)} %refs_0_.1, f32[4,8,512]{2,1,0:T(8,128)} %refs_1_.1, f32[4,8,512]{2,1,0:T(8,128)} %refs_2_.1, ...), custom_call_target="tpu_custom_call" | custom-call | tf_op jit(solution)/shard_map/step/pallas_call | solution.py:440
  23.9 0.8 %deliver.1 = (f32[4,8,512]{2,1,0:T(8,128)}, f32[4,8,512]{2,1,0:T(8,128)}, f32[4,8,512]{2,1,0:T(8,128)}, f32[4,8,512]{2,1,0:T(8,128)}, f32[4,8,512]{2,1,0:T(8,128)}, /*index=5*/f32[4,8,512]{2,1,0:T(8,128)}) custom-call(f32[4,8,512]{2,1,0:T(8,128)S(1)} %get-tuple-element.12.refs_0_, f32[4,8,512]{2,1,0:T(8,128)S(1)} %get-tuple-element.13.refs_1_, ...), custom_call_target="tpu_custom_call" | custom-call | tf_op jit(solution)/shard_map/deliver/pallas_call | solution.py:460

commit v3 on v2

--- a/solution.py
+++ b/solution.py
@@ -92,7 +92,7 @@
     o_ex, o_ey, o_ez, o_hx, o_hy, o_hz,
     y_mat, z_mat, y_mat_in, z_mat_in,
     y_src, z_src, y_src_in, z_src_in,
-    y_out, z_out, y_back, z_back,
+    y_out, z_out, y_back,
     face_z, halo_y, halo_z,
     y_alpha, y_beta, z_alpha, z_beta, z_fwd, z_bwd,
     x_fac, y_fac, z_fac,
@@ -158,7 +158,8 @@
             peer = lax.rem(me + d, count)
             copies.append(
                 pltpu.make_async_remote_copy(
-                    src_ref=source.at[peer], dst_ref=target.at[me],
+                    src_ref=source.at[peer] if axis == "row" else source,
+                    dst_ref=target.at[me],
                     send_sem=send.at[step, d - 1], recv_sem=recv.at[step, d - 1],
                     device_id=(peer, c) if axis == "row" else (r, peer),
                     device_id_type=MESH,
@@ -166,7 +167,7 @@
             )
         for copy in copies:
             copy.start()
-        target[me] = source[me]
+        target[me] = source[me] if axis == "row" else source[...]
         sent.extend(copies)
         return copies
 
@@ -219,10 +220,9 @@
     z_beta[...] = beta
     left = jnp.sum(jnp.where(first, ground, alpha * here), axis=1)
     tail = beta * here
-    for p in range(cols):
-        z_mat[p, 0:1, :] = alpha[p, nz - 1 :, :]
-        z_mat[p, 1:2, :] = left[p : p + 1]
-        z_mat[p, 2:3, :] = tail[p, nz - 1 :, :]
+    z_mat[0] = alpha[:, nz - 1, :]
+    z_mat[1] = left
+    z_mat[2] = tail[:, nz - 1, :]
     z_mat_copies = exchange(0, "col", z_mat, z_mat_in)
     forward = jnp.where(first, 0.0, roll_to(beta, 1, 1))
     backward = jnp.where(spot == nz - 1, 0.0, beta)
@@ -272,14 +272,13 @@
         return charge, left, right
 
     def send_z(stage, left, right):
-        for p in range(cols):
-            z_src[stage, p, 0:1, :] = left[p : p + 1]
-            z_src[stage, p, 1:2, :] = right[p, nz - 1 :, :]
+        z_src[stage, 0] = left
+        z_src[stage, 1] = right[:, nz - 1, :]
         return exchange(1 + 2 * stage, "col", z_src.at[stage], z_src_in.at[stage])
 
     def expand_z(stage, charge):
-        near = jnp.stack([z_back[stage, p, 0:1, :] for p in range(cols)], 0)
-        beyond = jnp.stack([z_back[stage, p, 1:2, :] for p in range(cols)], 0)
+        near = z_out[stage, c][:, None, :]
+        beyond = z_out[stage, c + 1][:, None, :]
         cells = z_alpha[...] * near + z_beta[...] * charge
         cells = cells + jnp.where(spot == nz - 1, z_beta[...] * beyond, 0.0)
         cells = jnp.where(first, near, cells)
@@ -360,23 +359,36 @@
     arrive(y_mat_copies)
     y_inverse = line_factors(y_mat_in, rows, keeper(y_fac))
     arrive(z_mat_copies)
-    z_inverse = line_factors(z_mat_in, cols, keeper(z_fac))
+    grounded = z_mat_in[0, 1]
+    for q in range(cols):
+        link = z_mat_in[q, 0]
+        inverse = 1.0 / (grounded + link)
+        z_fac[0, q] = link * inverse
+        z_fac[1, q] = inverse
+        if q < cols - 1:
+            grounded = z_mat_in[q + 1, 1] + z_mat_in[q, 2] + link * inverse * grounded
 
     def half_lines(stage, y_copies, z_copies):
         arrive(y_copies)
         line_solve(stage, y_src_in, rows, loader(y_fac), y_inverse, y_out)
         y_returns = exchange(2 + 2 * stage, "row", y_out.at[stage], y_back.at[stage])
         arrive(z_copies)
-        line_solve(stage, z_src_in, cols, loader(z_fac), z_inverse, z_out)
-        z_returns = exchange(2 + 2 * stage, "col", z_out.at[stage], z_back.at[stage])
-        return y_returns, z_returns
-
-    y_returns, z_returns = half_lines(0, y_copies, z_copies)
+        source = [z_src_in[stage, 0, 0]]
+        for q in range(1, cols):
+            own = z_src_in[stage, q, 0] + z_src_in[stage, q - 1, 1]
+            source.append(own + z_fac[0, q - 1] * source[-1])
+        value = jnp.zeros((ny, nx), jnp.float32)
+        z_out[stage, cols] = value
+        for q in range(cols - 1, -1, -1):
+            value = z_fac[1, q] * source[q] + z_fac[0, q] * value
+            z_out[stage, q] = value
+        return y_returns
+
+    y_returns = half_lines(0, y_copies, z_copies)
 
     arrive(y_returns)
     half_ex, beyond_ex = expand_y(0, y_charge)
     slope_ex = up_y(half_ex, beyond_ex)
-    arrive(z_returns)
     half_ey, beyond_ey = expand_z(0, z_charge)
     slope_ey = up_z(half_ey, beyond_ey)
 
@@ -389,7 +401,7 @@
     body = lossless * half_ey + lossy * ey[...]
     mean_ey = chain_solve(loader(x_fac), x_inverse, body - down_x(slope_ex), 2)
     next_ey = 2.0 * mean_ey - ey[...]
-    y_returns, z_returns = half_lines(1, y_copies, z_copies)
+    y_returns = half_lines(1, y_copies, z_copies)
     o_ey[...] = next_ey
     o_hz[...] = STEP * (flux_of_z + 2.0 * slope_ex - up_x(next_ey))
 
@@ -399,7 +411,6 @@
     o_ez[...] = next_ez
     above = 2.0 * beyond_ez - halo_y[0:1]
     o_hx[...] = STEP * (flux_of_x + 2.0 * slope_ey - up_y(next_ez, above))
-    arrive(z_returns)
     mean_ex, beyond_ex = expand_z(1, z_charge)
     next_ex = 2.0 * mean_ex - ex[...]
     o_ex[...] = next_ex
@@ -427,15 +438,15 @@
     ny, nz, nx = fields[0].shape
     f32 = jnp.float32
     block = (ny, nz, nx)
-    y_levels, z_levels = len(levels_of(8)), len(levels_of(8))
+    y_levels = len(levels_of(8))
     scratch = [
-        (rows, 3, nx), (cols, 3, nx), (rows, 3, nx), (cols, 3, nx),
-        (2, rows, 2, nx), (2, cols, 2, nx), (2, rows, 2, nx), (2, cols, 2, nx),
-        (2, rows, 2, nx), (2, cols, 2, nx), (2, rows, 2, nx), (2, cols, 2, nx),
+        (rows, 3, nx), (3, ny, nx), (rows, 3, nx), (cols, 3, ny, nx),
+        (2, rows, 2, nx), (2, 2, ny, nx), (2, rows, 2, nx), (2, cols, 2, ny, nx),
+        (2, rows, 2, nx), (2, cols + 1, ny, nx), (2, rows, 2, nx),
         (2, ny, 1, nx), (2, nz, nx), (2, ny, 1, nx),
         block, block, block, block,
         (len(levels_of(nz)),) + block, (len(levels_of(nz)),) + block,
-        (2 * len(levels_of(nx)),) + block, (2 * y_levels, 8, nx), (2 * z_levels, 8, nx),
+        (2 * len(levels_of(nx)),) + block, (2 * y_levels, 8, nx), (2, cols, ny, nx),
     ]
     held = pl.pallas_call(
         functools.partial(kernel, rows, cols),

time: 24.9 us -> 22.2 us (0.89)
  Pallas kernels: 24.1 us -> 21.4 us
    pallas_call x1, Pallas kernels: 23.3 us -> 20.6 us  [fused(): pl.pallas_call(functools.partial(kernel, rows, cols), out_shape=[pltpu.VM...]
where the time goes in v3:
time: 22.2 us; the launch traced here: 22 us
  Pallas kernels  21.4 us (96%)
  between operations  0.64 us (3%)
    pallas_call x1, Pallas kernels, fused(): pl.pallas_call(functools.partial(kernel, rows, cols), out_shape=[pltpu.VM...  20.6 us
    pallas_call x1, Pallas kernels, fused(): pl.pallas_call(deliver, out_shape=[jax.ShapeDtypeStruct(block, f32)] * 6,...  0.79 us

profile of v3, /device:TPU:0, one launch (start us, length us, event | category | flops | bytes accessed | tf_op | source)
XLA Modules:
  0.0 22.0 jit_solution(434675006524774493)
XLA Ops:
  0.6 20.6 %step.1 = (f32[4,8,512]{2,1,0:T(8,128)S(1)}, f32[4,8,512]{2,1,0:T(8,128)S(1)}, f32[4,8,512]{2,1,0:T(8,128)S(1)}, f32[4,8,512]{2,1,0:T(8,128)S(1)}, f32[4,8,512]{2,1,0:T(8,128)S(1)}, /*index=5*/f32[4,8,512]{2,1,0:T(8,128)S(1)}) custom-call(f32[4,8,512]{2,1,0:T(8,128)} %refs_0_.1, f32[4,8,512]{2,1,0:T(8,128)} %refs_1_.1, f32[4,8,512]{2,1,0:T(8,128)} %refs_2_.1, ...), custom_call_target="tpu_custom_call" | custom-call | tf_op jit(solution)/shard_map/step/pallas_call | solution.py:451
  21.3 0.8 %deliver.1 = (f32[4,8,512]{2,1,0:T(8,128)}, f32[4,8,512]{2,1,0:T(8,128)}, f32[4,8,512]{2,1,0:T(8,128)}, f32[4,8,512]{2,1,0:T(8,128)}, f32[4,8,512]{2,1,0:T(8,128)}, /*index=5*/f32[4,8,512]{2,1,0:T(8,128)}) custom-call(f32[4,8,512]{2,1,0:T(8,128)S(1)} %get-tuple-element.12.refs_0_, f32[4,8,512]{2,1,0:T(8,128)S(1)} %get-tuple-element.13.refs_1_, ...), custom_call_target="tpu_custom_call" | custom-call | tf_op jit(solution)/shard_map/deliver/pallas_call | solution.py:471

commit v4 on v3

--- a/solution.py
+++ b/solution.py
@@ -368,10 +368,11 @@
         if q < cols - 1:
             grounded = z_mat_in[q + 1, 1] + z_mat_in[q, 2] + link * inverse * grounded
 
-    def half_lines(stage, y_copies, z_copies):
+    def half_lines(stage, y_copies, z_copies, between):
         arrive(y_copies)
         line_solve(stage, y_src_in, rows, loader(y_fac), y_inverse, y_out)
         y_returns = exchange(2 + 2 * stage, "row", y_out.at[stage], y_back.at[stage])
+        between()
         arrive(z_copies)
         source = [z_src_in[stage, 0, 0]]
         for q in range(1, cols):
@@ -384,29 +385,31 @@
             z_out[stage, q] = value
         return y_returns
 
-    y_returns = half_lines(0, y_copies, z_copies)
-
+    y_returns = half_lines(0, y_copies, z_copies, lambda: None)
+
+    half_ey, beyond_ey = expand_z(0, z_charge)
+    slope_ey = up_z(half_ey, beyond_ey)
+
+    lossless = eps[...] * (1.0 / AREA)
+    lossy = sig[...] * (SIDE / AREA)
+    late_charge, left, right = reduce_y(lossless * half_ez + lossy * ez[...], -slope_ey)
+    y_copies = send_y(1, left, right)
     arrive(y_returns)
     half_ex, beyond_ex = expand_y(0, y_charge)
     slope_ex = up_y(half_ex, beyond_ex)
-    half_ey, beyond_ey = expand_z(0, z_charge)
-    slope_ey = up_z(half_ey, beyond_ey)
-
-    lossless = eps[...] * (1.0 / AREA)
-    lossy = sig[...] * (SIDE / AREA)
-    y_charge, left, right = reduce_y(lossless * half_ez + lossy * ez[...], -slope_ey)
-    y_copies = send_y(1, left, right)
     z_charge, left, right = reduce_z(lossless * half_ex + lossy * ex[...], -slope_ez)
     z_copies = send_z(1, left, right)
-    body = lossless * half_ey + lossy * ey[...]
-    mean_ey = chain_solve(loader(x_fac), x_inverse, body - down_x(slope_ex), 2)
-    next_ey = 2.0 * mean_ey - ey[...]
-    y_returns = half_lines(1, y_copies, z_copies)
-    o_ey[...] = next_ey
-    o_hz[...] = STEP * (flux_of_z + 2.0 * slope_ex - up_x(next_ey))
-
+
+    def solve_ey():
+        body = lossless * half_ey + lossy * ey[...]
+        mean_ey = chain_solve(loader(x_fac), x_inverse, body - down_x(slope_ex), 2)
+        next_ey = 2.0 * mean_ey - ey[...]
+        o_ey[...] = next_ey
+        o_hz[...] = STEP * (flux_of_z + 2.0 * slope_ex - up_x(next_ey))
+
+    y_returns = half_lines(1, y_copies, z_copies, solve_ey)
     arrive(y_returns)
-    mean_ez, beyond_ez = expand_y(1, y_charge)
+    mean_ez, beyond_ez = expand_y(1, late_charge)
     next_ez = 2.0 * mean_ez - ez[...]
     o_ez[...] = next_ez
     above = 2.0 * beyond_ez - halo_y[0:1]

time: 22.2 us -> 21 us (0.946)
  Pallas kernels: 21.4 us -> 20.1 us
    pallas_call x1, Pallas kernels: 20.6 us -> 19.3 us  [fused(): pl.pallas_call(functools.partial(kernel, rows, cols), out_shape=[pltpu.VM...]
where the time goes in v4:
time: 21 us; the launch traced here: 20.8 us
  Pallas kernels  20.1 us (96%)
  between operations  0.64 us (3%)
    pallas_call x1, Pallas kernels, fused(): pl.pallas_call(functools.partial(kernel, rows, cols), out_shape=[pltpu.VM...  19.3 us
    pallas_call x1, Pallas kernels, fused(): pl.pallas_call(deliver, out_shape=[jax.ShapeDtypeStruct(block, f32)] * 6,...  0.79 us

profile of v4, /device:TPU:0, one launch (start us, length us, event | category | flops | bytes accessed | tf_op | source)
XLA Modules:
  0.0 20.8 jit_solution(9698717873668659700)
XLA Ops:
  0.6 19.3 %step.1 = (f32[4,8,512]{2,1,0:T(8,128)S(1)}, f32[4,8,512]{2,1,0:T(8,128)S(1)}, f32[4,8,512]{2,1,0:T(8,128)S(1)}, f32[4,8,512]{2,1,0:T(8,128)S(1)}, f32[4,8,512]{2,1,0:T(8,128)S(1)}, /*index=5*/f32[4,8,512]{2,1,0:T(8,128)S(1)}) custom-call(f32[4,8,512]{2,1,0:T(8,128)} %refs_0_.1, f32[4,8,512]{2,1,0:T(8,128)} %refs_1_.1, f32[4,8,512]{2,1,0:T(8,128)} %refs_2_.1, ...), custom_call_target="tpu_custom_call" | custom-call | tf_op jit(solution)/shard_map/step/pallas_call | solution.py:454
  20.0 0.8 %deliver.1 = (f32[4,8,512]{2,1,0:T(8,128)}, f32[4,8,512]{2,1,0:T(8,128)}, f32[4,8,512]{2,1,0:T(8,128)}, f32[4,8,512]{2,1,0:T(8,128)}, f32[4,8,512]{2,1,0:T(8,128)}, /*index=5*/f32[4,8,512]{2,1,0:T(8,128)}) custom-call(f32[4,8,512]{2,1,0:T(8,128)S(1)} %get-tuple-element.12.refs_0_, f32[4,8,512]{2,1,0:T(8,128)S(1)} %get-tuple-element.13.refs_1_, ...), custom_call_target="tpu_custom_call" | custom-call | tf_op jit(solution)/shard_map/deliver/pallas_call | solution.py:474
